TPU v7x, 32 devices: a whole 2x2x4 slice. The times are simulated.
32 devices in a mesh: section: 2 (over x), tile: 16 (over z, y, core).
Axes of the slice: x: 2, y: 2, z: 4, core: 2. Of those that a mesh axis runs over, the one named last changes fastest.
Arguments:
- coarse: bfloat16 [12, 512, 128], P(None, 'tile'), may hold values from -6 to 6
- lift_weight: bfloat16 [128, 12], replicated, may hold values from -1.75 to 1.75
- conv_weight: bfloat16 [3, 3, 128, 128], replicated, may hold values from -0.1875 to 0.1875
- out_weight: bfloat16 [4, 128], replicated, may hold values from -0.5 to 0.5
- denoise_in: bfloat16 [128, 8], replicated, may hold values from -2 to 2
- denoise_mid: bfloat16 [128, 128], replicated, may hold values from -0.5 to 0.5
- denoise_out: bfloat16 [4, 128], replicated, may hold values from -0.5 to 0.5
- base_noise: bfloat16 [4, 4, 512, 128], P(None, None, 'tile'), may hold values from -5 to 5
- slot_noise: bfloat16 [4, 4, 512, 128], P(None, None, 'tile'), may hold values from -5 to 5
- extra_dest: int32 [16, 8], P('tile'), may hold values from -1 to 15, as said below
Outputs:
- moments: float32 [2, 4, 512, 128], P('section', None, 'tile')
Inputs may be any that keep to these rules, and one draw needn't show every extreme that they name: `extra_dest`: the non-negative entries of row t come first and are consecutive device indices t + o, t + o + 1, ... (modulo 16) with 0 <= o and all of them within t to t + 8 - 1 modulo 16; the rest are -1. Every device is named exactly 4 times over all rows; some row has 8 non-negative entries.
All inputs are finite; a program needn't handle non-finite values.
Results may differ from a plain program's by a relative error of at most 0.0024.
Values may be sent and summed in bfloat16 or wider, within the bound.
No kernel may reach another device: no remote copies, remote signals or barrier semaphores. Data moves between devices by JAX's collectives and lax.ppermute only.
A program may use at most 64 MiB of HBM per device.

v0:
```python
import functools
import math

import jax
import jax.numpy as jnp
from jax import lax
from jax.experimental import pallas as pl
from jax.experimental.pallas import tpu as pltpu
from jax.sharding import PartitionSpec as P

NSTEP = 6
SIGMA_MAX = 4.0
SIGMA_MIN = 0.25
PLAN_POWER = 7.0
SECTIONS = 2
REACH = 8
VMEM_LIMIT = 40 * 1024 * 1024


def sigma_table(step_count):
    upper_root = SIGMA_MAX ** (1.0 / PLAN_POWER)
    lower_root = SIGMA_MIN ** (1.0 / PLAN_POWER)
    values = []
    for position in range(step_count):
        fraction = position / (step_count - 1)
        values.append((upper_root + fraction * (lower_root - upper_root)) ** PLAN_POWER)
    values.append(0.0)
    return values


def step_table():
    sigmas = sigma_table(NSTEP)
    steps = []
    for now, after in zip(sigmas[:-1], sigmas[1:]):
        scale = 1.0 / math.sqrt(now * now + 1.0)
        skip = 1.0 / (now * now + 1.0)
        rate = (after - now) / now
        steps.append((scale, 1.0 + rate * (1.0 - skip), -rate * now * scale))
    return sigmas[0], steps


def half_silu(half):
    return (half * jnp.tanh(half) + half).astype(jnp.bfloat16)


def dot(left, right):
    return jnp.dot(left, right, preferred_element_type=jnp.float32)


def halved(weight):
    return (0.5 * weight.astype(jnp.float32)).astype(jnp.bfloat16)


def denoise(noise, condition, w_in, w_mid, w_out):
    start, steps = step_table()
    latent = start * noise
    for scale, keep, gain in steps:
        stacked = jnp.concatenate([(scale * latent).astype(jnp.bfloat16), condition], axis=0)
        hidden = half_silu(dot(w_in, stacked))
        hidden = half_silu(dot(w_mid, hidden))
        latent = keep * latent + gain * dot(w_out, hidden)
    return condition.astype(jnp.float32) + latent


def flat(field):
    return field.astype(jnp.float32).reshape(field.shape[0], -1)


def regress_kernel(coarse_ref, edge_ref, lift_ref, conv_ref, out_ref, condition_ref):
    section = lax.axis_index("section")
    channels_in, rows_all, width = coarse_ref.shape
    rows = rows_all // SECTIONS
    coarse = coarse_ref[...].astype(jnp.float32)
    edge = edge_ref[...].astype(jnp.float32)
    upper = jnp.concatenate([edge, coarse[:, : rows + 1]], axis=1)
    lower = jnp.concatenate([coarse[:, rows - 1 :], edge], axis=1)
    window = jnp.where(section == 0, upper, lower)
    window = window.reshape(channels_in, (rows + 2) * width).astype(jnp.bfloat16)
    half = dot(halved(lift_ref[...]), window)
    lifted = half * jnp.tanh(half) + half
    channels = lifted.shape[0]
    column = lax.broadcasted_iota(jnp.int32, (channels, width), 1)
    taps = []
    for row in range(rows + 2):
        piece = lifted[:, row * width : (row + 1) * width]
        left = jnp.where(column == 0, 0.0, pltpu.roll(piece, 1, 1))
        right = jnp.where(column == width - 1, 0.0, pltpu.roll(piece, width - 1, 1))
        taps.append(jnp.concatenate([left, piece, right], axis=0).astype(jnp.bfloat16))
    stacked = jnp.concatenate(taps, axis=1)
    half = None
    for tap in range(3):
        weight = halved(conv_ref[tap].reshape(3 * channels, channels))
        part = lax.dot_general(
            weight,
            stacked[:, tap * width : (tap + rows) * width],
            (((0,), (0,)), ((), ())),
            preferred_element_type=jnp.float32,
        )
        half = part if half is None else half + part
    condition_ref[...] = dot(out_ref[...], half_silu(half)).astype(jnp.bfloat16)


def base_kernel(noise_ref, condition_ref, in_ref, mid_ref, out_ref, sums_ref):
    section = lax.axis_index("section")
    members, channels, rows_all, width = noise_ref.shape
    rows = rows_all // SECTIONS
    condition = condition_ref[...]
    noise = []
    for member in range(members):
        upper = noise_ref[member, :, :rows]
        lower = noise_ref[member, :, rows:]
        noise.append(flat(jnp.where(section == 0, upper, lower)))
    samples = denoise(
        jnp.concatenate(noise, axis=1),
        jnp.concatenate([condition] * members, axis=1),
        halved(in_ref[...]),
        halved(mid_ref[...]),
        out_ref[...],
    )
    cells = rows * width
    pieces = [samples[:, m * cells : (m + 1) * cells] for m in range(members)]
    sums_ref[0] = functools.reduce(lambda a, b: a + b, pieces)
    sums_ref[1] = functools.reduce(lambda a, b: a + b, [p * p for p in pieces])


def slot_kernel(
    routes_ref,
    near_ref,
    far2_ref,
    far4_ref,
    far6_ref,
    far8_ref,
    mine_ref,
    theirs_ref,
    base_ref,
    in_ref,
    mid_ref,
    out_ref,
    own_ref,
    peer_ref,
    noise_ref,
    sample_ref,
    where_ref,
):
    tile = lax.axis_index("tile")
    tiles = lax.axis_size("tile")
    core = lax.rem(tile, 2)
    chip_tile = tile - core
    records = (near_ref, far2_ref, far4_ref, far6_ref, far8_ref)
    channels, cells = mine_ref.shape
    rows, width = noise_ref.shape[2:]

    def names(table, device):
        first = routes_ref[table * REACH]
        place = lax.rem(device - first + tiles, tiles)
        entry = routes_ref[table * REACH + jnp.minimum(place, REACH - 1)]
        return (first >= 0) & (place < REACH) & (entry >= 0)

    def members_of(table):
        return 4 + sum((routes_ref[table * REACH + j] >= 0).astype(jnp.int32) for j in range(REACH))

    own_row = REACH + core
    peer_row = REACH + 1 - core
    found = []
    for step in range(5):
        device_row = own_row + 2 * step
        device = lax.rem(tile + 2 * step, tiles)
        source_tiles, named = [], []
        for back in range(REACH):
            row = device_row - back
            source_tiles.append(lax.rem(chip_tile + row - REACH + tiles, tiles))
            named.append(names(row, device))
        for side, row in ((0, own_row), (1, peer_row)):
            back = device_row - row
            inside = (back >= 0) & (back < REACH)
            target = lax.rem(chip_tile + row - REACH, tiles)
            live = jnp.int32(0)
            rank = jnp.int32(0)
            for at in range(REACH):
                live = live | ((back == at) & named[at]).astype(jnp.int32)
                rank = rank + (named[at] & (source_tiles[at] < target)).astype(jnp.int32)
            found.append((step, side, inside & (live == 1), rank))

    count = jnp.int32(0)
    for step, side, live, rank in found:
        place = count

        @pl.when(live)
        def _():
            noise_ref[place] = records[step][pl.ds(channels * rank, channels)]
            where_ref[place] = side

        count = count + live.astype(jnp.int32)

    own_scale = 1.0 / members_of(own_row).astype(jnp.float32)
    peer_scale = 1.0 / members_of(peer_row).astype(jnp.float32)
    sample_ref[0] = base_ref[...]
    sample_ref[1] = jnp.zeros_like(base_ref)
    w_in, w_mid, w_out = halved(in_ref[...]), halved(mid_ref[...]), out_ref[...]
    group = 2

    @pl.loop(0, (count + group - 1) // group)
    def _(turn):
        noise, conditions, sides = [], [], []
        for member in range(group):
            place = group * turn + member
            side = where_ref[jnp.minimum(place, count - 1)]
            sides.append(side)
            noise.append(flat(noise_ref[place]))
            conditions.append(jnp.where(side == 0, mine_ref[...], theirs_ref[...]))
        samples = denoise(
            jnp.concatenate(noise, axis=1), jnp.concatenate(conditions, axis=1), w_in, w_mid, w_out
        )
        for member in range(group):
            live = group * turn + member < count
            sample = samples[:, member * cells : (member + 1) * cells]
            sample = jnp.where(live, sample, 0.0)
            sample_ref[sides[member], 0] += sample
            sample_ref[sides[member], 1] += sample * sample

    for moment in range(2):
        own_ref[moment] = (own_scale * sample_ref[0, moment]).reshape(channels, rows, width)
        peer_ref[moment] = (peer_scale * sample_ref[1, moment]).reshape(channels, rows, width)


def in_vmem(count):
    return [pl.BlockSpec(memory_space=pltpu.VMEM)] * count


def from_ahead(block, distance):
    count = lax.axis_size("tile")
    return lax.ppermute(block, "tile", [((i + distance) % count, i) for i in range(count)])


def swap_cores(block):
    count = lax.axis_size("tile")
    return lax.ppermute(block, "tile", [(i, i ^ 1) for i in range(count)])


def swap_sections(block):
    return lax.ppermute(block, "section", [(0, 1), (1, 0)])


def edge_rows(coarse, section):
    count = lax.axis_size("tile")
    pairs = [(t, t + 1) for t in range(count - 1)]
    pairs += [(count + t + 1, count + t) for t in range(count - 1)]
    last = coarse[:, -1:]
    first = coarse[:, :1]
    return lax.ppermute(jnp.where(section == 0, last, first), ("section", "tile"), pairs)


def body(
    coarse,
    lift_weight,
    conv_weight,
    out_weight,
    denoise_in,
    denoise_mid,
    denoise_out,
    base_noise,
    slot_noise,
    extra_dest,
):
    section = lax.axis_index("section")
    tile = lax.axis_index("tile")
    count = lax.axis_size("tile")
    slots, channels, rows_all, width = slot_noise.shape
    members = base_noise.shape[0]
    rows = rows_all // SECTIONS
    cells = rows * width
    hidden = denoise_mid.shape[0]
    step_flops = 2 * NSTEP * hidden * (hidden + 3 * channels)
    params = pltpu.CompilerParams(vmem_limit_bytes=VMEM_LIMIT)

    edge = edge_rows(coarse, section)
    half_noise = lax.dynamic_slice_in_dim(slot_noise, rows * section, rows, axis=2)
    half_noise = half_noise.reshape(slots * channels, rows, width)
    far8_noise = from_ahead(half_noise, 8)
    far8_routes = from_ahead(extra_dest, 8)

    condition = pl.pallas_call(
        regress_kernel,
        out_shape=jax.ShapeDtypeStruct((channels, cells), jnp.bfloat16),
        in_specs=in_vmem(5),
        out_specs=pl.BlockSpec(memory_space=pltpu.VMEM),
        compiler_params=params,
        cost_estimate=pl.CostEstimate(
            flops=2 * cells * hidden * (9 * hidden + 16),
            bytes_accessed=600_000,
            transcendentals=2 * cells * hidden,
        ),
        name="regression",
    )(coarse, edge, lift_weight, conv_weight, out_weight)

    pair = jnp.concatenate([extra_dest, far8_routes], axis=0).astype(jnp.bfloat16)
    pair = jnp.pad(pair, ((0, rows - 2), (0, width - REACH)))
    record = jnp.concatenate([half_noise, pair[None]], axis=0)
    far2, far4, far6 = [from_ahead(record, distance) for distance in (2, 4, 6)]
    got = [r[-1, :2, :REACH].astype(jnp.int32) for r in (far2, far4, far6)]
    if count == 2 * REACH:
        behind = [far8_routes[0], got[0][1], got[1][1], got[2][1]]
    else:
        behind = [from_ahead(extra_dest, -distance)[0] for distance in (8, 6, 4, 2)]
    ahead = [extra_dest[0], got[0][0], got[1][0], got[2][0], far8_routes[0]]
    own_routes = jnp.stack(behind + ahead)
    peer_condition = swap_cores(condition)
    peer_routes = swap_cores(own_routes)
    even = jnp.where(tile % 2 == 0, own_routes, peer_routes)
    odd = jnp.where(tile % 2 == 0, peer_routes, own_routes)
    routes = jnp.stack([even, odd], axis=1).reshape(-1)

    base = pl.pallas_call(
        base_kernel,
        out_shape=jax.ShapeDtypeStruct((2, channels, cells), jnp.float32),
        in_specs=in_vmem(5),
        out_specs=pl.BlockSpec(memory_space=pltpu.VMEM),
        compiler_params=params,
        cost_estimate=pl.CostEstimate(
            flops=members * cells * step_flops,
            bytes_accessed=400_000,
            transcendentals=2 * NSTEP * members * cells * hidden,
        ),
        name="base_members",
    )(base_noise, condition, denoise_in, denoise_mid, denoise_out)

    moments = jax.ShapeDtypeStruct((2, channels, rows, width), jnp.float32)
    own, peer = pl.pallas_call(
        slot_kernel,
        out_shape=(moments, moments),
        in_specs=[pl.BlockSpec(memory_space=pltpu.SMEM)] + in_vmem(11),
        out_specs=(pl.BlockSpec(memory_space=pltpu.VMEM),) * 2,
        scratch_shapes=[
            pltpu.VMEM((2 * 5, channels, rows, width), jnp.bfloat16),
            pltpu.VMEM((2, 2, channels, cells), jnp.float32),
            pltpu.SMEM((2 * 5,), jnp.int32),
        ],
        compiler_params=params,
        cost_estimate=pl.CostEstimate(
            flops=slots * cells * step_flops,
            bytes_accessed=1_000_000,
            transcendentals=2 * NSTEP * slots * cells * hidden,
        ),
        name="slot_members",
    )(
        routes,
        half_noise,
        far2,
        far4,
        far6,
        far8_noise,
        condition,
        peer_condition,
        base,
        denoise_in,
        denoise_mid,
        denoise_out,
    )
    total = own + swap_cores(peer)
    mean = total[0]
    variance = total[1] - mean * mean
    kept = jnp.where(section == 0, mean, variance)
    sent = jnp.where(section == 0, variance, mean)
    received = swap_sections(sent)
    upper = jnp.where(section == 0, kept, received)
    lower = jnp.where(section == 0, received, kept)
    return jnp.concatenate([upper, lower], axis=1)[None]


def solution(mesh):
    in_specs = (
        P(None, "tile", None),
        P(),
        P(),
        P(),
        P(),
        P(),
        P(),
        P(None, None, "tile", None),
        P(None, None, "tile", None),
        P("tile", None),
    )
    out_specs = P("section", None, "tile", None)
    return jax.shard_map(body, mesh=mesh, in_specs=in_specs, out_specs=out_specs, check_vma=False)
```

profile of v0, /device:TPU:0, one launch (start us, length us, event | category | flops | bytes accessed | tf_op | source)
XLA Modules:
  0.0 47.8 jit_solution(104473473068010144)
XLA Ops:
  0.0 0.0 copy-start
  0.0 0.0 copy-start.9
  0.0 4.0 %collective-permute-start = (s32[1,8]{1,0:T(1,128)}, s32[1,8]{1,0:T(1,128)S(1)}, u32[]{:S(2)}, u32[]{:S(2)}) collective-permute-start(s32[1,8]{1,0:T(1,128)} %param.19), channel_id=1, source_target_pairs={{8,0},{9,1},{10,2},{11,3},{12,4},{13,5},{14,6},{15,7},{0,8},{1,9},... | collective-permute-start | bytes 104 | tf_op jit(solution)/shard_map/ppermute | solution.py:232
  4.0 0.0 copy-done.9
  4.0 0.0 copy-done
  4.1 0.0 copy-start.1
  4.1 1.6 %collective-permute-done = s32[1,8]{1,0:T(1,128)S(1)} collective-permute-done((s32[1,8]{1,0:T(1,128)}, s32[1,8]{1,0:T(1,128)S(1)}, u32[]{:S(2)}, u32[]{:S(2)}) %collective-permute-start) | collective-permute-done | bytes 64 | tf_op jit(solution)/shard_map/ppermute | solution.py:232
  5.8 3.9 %collective-permute-start.3 = (bf16[17,16,128]{2,1,0:T(8,128)(2,1)S(1)}, bf16[17,16,128]{2,1,0:T(8,128)(2,1)S(1)}, u32[]{:S(2)}, u32[]{:S(2)}) collective-permute-start(bf16[17,16,128]{2,1,0:T(8,128)(2,1)S(1)} %pad_maximum_fusion), channel_id=1, source_target_pairs={{6,0},{7,1},{8,2},{9,3},{10,4},{11,5},{12,6},{13,7},{14,8},{15,9},... | collective-permute-start | bytes 208904 | tf_op jit(solution)/shard_map/ppermute | solution.py:232
  9.7 0.0 copy-done.1
  9.7 1.3 %collective-permute-start.6 = (bf16[12,1,128]{2,1,0:T(2,128)(2,1)S(1)}, bf16[12,1,128]{2,1,0:T(2,128)(2,1)S(1)}, u32[]{:S(2)}, u32[]{:S(2)}) collective-permute-start(bf16[12,1,128]{2,1,0:T(2,128)(2,1)S(1)} %broadcast_select_fusion.2), channel_id=1, source_target_pairs={{0,1},{1,2},{2,3},{3,4},{4,5},{5,6},{6,7},{7,8},{8,9},{9,10},{10,1... | collective-permute-start | bytes 9224 | tf_op jit(solution)/shard_map/ppermute | solution.py:250
  11.0 1.0 %collective-permute-start.5 = (bf16[16,16,128]{2,1,0:T(8,128)(2,1)S(1)}, bf16[16,16,128]{2,1,0:T(8,128)(2,1)S(1)}, u32[]{:S(2)}, u32[]{:S(2)}) collective-permute-start(bf16[16,16,128]{2,1,0:T(8,128)(2,1)S(1)} %bitcast.42), channel_id=1, source_target_pairs={{8,0},{9,1},{10,2},{11,3},{12,4},{13,5},{14,6},{15,7},{0,8},{1,9},... | collective-permute-start | bytes 196616 | tf_op jit(solution)/shard_map/ppermute | solution.py:232
  12.0 0.0 copy-start.8
  12.0 0.7 %copy-done.8 = bf16[128,8]{0,1:T(8,128)(2,1)S(1)} copy-done((bf16[128,8]{0,1:T(8,128)(2,1)S(1)}, bf16[128,8]{0,1:T(8,128)(2,1)}, u32[]{:S(2)}) %copy-start.8) | copy-done | bytes 2072
  12.7 0.0 copy-start.7
  12.7 0.1 copy.20.in_ref
  12.8 0.6 %copy-done.7 = bf16[128,12]{0,1:T(8,128)(2,1)S(1)} copy-done((bf16[128,12]{0,1:T(8,128)(2,1)S(1)}, bf16[128,12]{0,1:T(8,128)(2,1)}, u32[]{:S(2)}) %copy-start.7) | copy-done | bytes 3096
  13.4 0.0 copy-start.5
  13.4 0.1 copy.19.lift_ref
  13.5 3.6 %collective-permute-start.2 = (bf16[17,16,128]{2,1,0:T(8,128)(2,1)S(1)}, bf16[17,16,128]{2,1,0:T(8,128)(2,1)S(1)}, u32[]{:S(2)}, u32[]{:S(2)}) collective-permute-start(bf16[17,16,128]{2,1,0:T(8,128)(2,1)S(1)} %pad_maximum_fusion), channel_id=1, source_target_pairs={{4,0},{5,1},{6,2},{7,3},{8,4},{9,5},{10,6},{11,7},{12,8},{13,9},{1... | collective-permute-start | bytes 208904 | tf_op jit(solution)/shard_map/ppermute | solution.py:232
  17.2 1.4 %collective-permute-start.1 = (bf16[17,16,128]{2,1,0:T(8,128)(2,1)S(1)}, bf16[17,16,128]{2,1,0:T(8,128)(2,1)S(1)}, u32[]{:S(2)}, u32[]{:S(2)}) collective-permute-start(bf16[17,16,128]{2,1,0:T(8,128)(2,1)S(1)} %pad_maximum_fusion), channel_id=1, source_target_pairs={{2,0},{3,1},{4,2},{5,3},{6,4},{7,5},{8,6},{9,7},{10,8},{11,9},{12,... | collective-permute-start | bytes 208904 | tf_op jit(solution)/shard_map/ppermute | solution.py:232
  18.6 0.0 collective-permute-done.6.edge_ref
  18.6 0.0 copy-done.5
  18.6 0.0 copy-start.2
  18.6 1.0 %copy-done.2 = bf16[3,3,128,128]{3,2,1,0:T(8,128)(2,1)S(1)} copy-done((bf16[3,3,128,128]{3,2,1,0:T(8,128)(2,1)S(1)}, bf16[3,3,128,128]{3,2,1,0:T(8,128)(2,1)}, u32[]{:S(2)}) %copy-start.2) | copy-done | bytes 294936
  19.5 0.0 copy-start.3
  19.5 1.4 %regression.1.condition_ref.mine_ref = bf16[4,2048]{1,0:T(4,128)(2,1)S(1)} custom-call(bf16[12,32,128]{2,1,0:T(8,128)(2,1)S(1)} %copy-done.1, bf16[12,1,128]{2,1,0:T(2,128)(2,1)S(1)} %collective-permute-done.6.edge_ref, bf16[128,12]{1,0:T(8,128)(2,1)S(1)} %copy.19.lift_ref, bf16[3,3,128,128]{3,2,1,0:T(8,128)(2,1)S(1)} %copy-done.2, bf16[4,128]{1,0:T(4,128)(2,1)S(1)} %copy-done.5), custom_call_target="tpu_custom_call" | custom-call | flops 612368384 | bytes 600000 | tf_op jit(solution)/shard_map/regression/pallas_call | solution.py:282
  20.9 0.0 copy-start.4
  20.9 0.8 %collective-permute-start.7 = (bf16[4,2048]{1,0:T(4,128)(2,1)S(1)}, bf16[4,2048]{1,0:T(4,128)(2,1)S(1)}, u32[]{:S(2)}, u32[]{:S(2)}) collective-permute-start(bf16[4,2048]{1,0:T(4,128)(2,1)S(1)} %regression.1.condition_ref.mine_ref), channel_id=1, source_target_pairs={{0,1},{1,0},{2,3},{3,2},{4,5},{5,4},{6,7},{7,6},{8,9},{9,8},{10,11... | collective-permute-start | bytes 49160 | tf_op jit(solution)/shard_map/ppermute | solution.py:237
  21.8 0.0 collective-permute-done.3.far6_ref
  21.8 0.0 collective-permute-done.2.far4_ref
  21.8 0.0 collective-permute-done.1.far2_ref
  21.9 0.0 copy-start.6
  21.9 0.1 collective-permute-start.4
  22.0 0.0 copy-done.3
  22.0 0.0 copy-done.4
  22.0 0.5 %copy-done.6 = bf16[4,128]{1,0:T(4,128)(2,1)S(1)} copy-done((bf16[4,128]{1,0:T(4,128)(2,1)S(1)}, bf16[4,128]{1,0:T(4,128)(2,1)}, u32[]{:S(2)}) %copy-start.6) | copy-done | bytes 1048
  22.5 8.6 %base_members.1.base_ref = f32[2,4,2048]{2,1,0:T(4,128)S(1)} custom-call(bf16[4,4,32,128]{3,2,1,0:T(8,128)(2,1)S(1)} %copy-done.3, bf16[4,2048]{1,0:T(4,128)(2,1)S(1)} %regression.1.condition_ref.mine_ref, bf16[128,8]{1,0:T(8,128)(2,1)S(1)} %copy.20.in_ref, bf16[128,128]{1,0:T(8,128)(2,1)S(1)} %copy-done.4, bf16[4,128]{1,0:T(4,128)(2,1)S(1)} %copy-done.6), custom_call_target="tpu_custom_call" | custom-call | flops 1761607680 | bytes 400000 | tf_op jit(solution)/shard_map/base_members/pallas_call | solution.py:313
  31.1 0.0 collective-permute-done.4
  31.1 0.1 copy.16
  31.2 0.1 copy.17
  31.3 0.1 copy.18
  31.4 0.1 reshape.16.routes_ref
  31.5 0.0 collective-permute-done.7.theirs_ref
  31.5 0.0 collective-permute-done.5.far8_ref
  31.5 10.3 %slot_members.1 = (f32[2,4,16,128]{3,2,1,0:T(8,128)S(1)}, f32[2,4,16,128]{3,2,1,0:T(8,128)S(1)}) custom-call(s32[144]{0:T(256)S(1)} %reshape.16.routes_ref, bf16[16,16,128]{2,1,0:T(8,128)(2,1)S(1)} %bitcast.43, bf16[17,16,128]{2,1,0:T(8,128)(2,1)S(1)} %collective-permute-done.1.far2_ref, bf16[17,16,128]{2,1,0:T(8,128)(2,1)S(1)} %collective-permute-done.2.far4_ref, ...), custom_call_target="tpu_custom_call" | custom-call | flops 1761607680 | bytes 1000000 | tf_op jit(solution)/shard_map/slot_members/pallas_call | solution.py:328
  41.8 0.1 collective-permute-start.8
  41.9 1.2 %collective-permute-done.8 = f32[2,4,16,128]{3,2,1,0:T(8,128)S(1)} collective-permute-done((f32[2,4,16,128]{3,2,1,0:T(8,128)S(1)}, f32[2,4,16,128]{3,2,1,0:T(8,128)S(1)}, u32[]{:S(2)}, u32[]{:S(2)}) %collective-permute-start.8) | collective-permute-done | bytes 65568 | tf_op jit(solution)/shard_map/ppermute | solution.py:237
  43.2 1.2 %collective-permute-start.9 = (f32[4,16,128]{2,1,0:T(8,128)S(1)}, f32[4,16,128]{2,1,0:T(8,128)S(1)}, u32[]{:S(2)}, u32[]{:S(2)}) collective-permute-start(f32[4,16,128]{2,1,0:T(8,128)S(1)} %fusion.1), channel_id=1, source_target_pairs={{0,16},{16,0},{1,17},{17,1},{2,18},{18,2},{3,19},{19,3},{4,20},{20... | collective-permute-start | bytes 98312 | tf_op jit(solution)/shard_map/ppermute | solution.py:241
  44.4 2.8 %collective-permute-done.9 = f32[4,16,128]{2,1,0:T(8,128)S(1)} collective-permute-done((f32[4,16,128]{2,1,0:T(8,128)S(1)}, f32[4,16,128]{2,1,0:T(8,128)S(1)}, u32[]{:S(2)}, u32[]{:S(2)}) %collective-permute-start.9) | collective-permute-done | bytes 32800 | tf_op jit(solution)/shard_map/ppermute | solution.py:241
  47.2 0.6 %maximum_bitcast_fusion = f32[1,4,32,128]{3,2,1,0:T(8,128)} fusion(f32[4,16,128]{2,1,0:T(8,128)S(1)} %get-tuple-element.10, f32[4,16,128]{2,1,0:T(8,128)S(1)} %get-tuple-element.9), kind=kLoop, calls=%fused_computation.1 | loop fusion | flops 16384 | bytes 131072 | tf_op jit(solution)/shard_map/broadcast_in_dim | solution.py:367
  (18 shorter events, 0.2 us)
Async XLA Ops:
  0.0 4.1 %copy-start = (bf16[4,4,32,128]{3,2,1,0:T(8,128)(2,1)S(1)}, bf16[4,4,32,128]{3,2,1,0:T(8,128)(2,1)}, u32[]{:S(2)}) copy-start(bf16[4,4,32,128]{3,2,1,0:T(8,128)(2,1)} %param.18) | copy-start | bytes 393220
  0.0 4.0 %copy-start.9 = (s32[1,8]{1,0:T(1,128)S(1)}, s32[1,8]{1,0:T(1,128)}, u32[]{:S(2)}) copy-start(s32[1,8]{1,0:T(1,128)} %param.19) | copy-start | bytes 100
  0.0 5.7 %collective-permute-start = (s32[1,8]{1,0:T(1,128)}, s32[1,8]{1,0:T(1,128)S(1)}, u32[]{:S(2)}, u32[]{:S(2)}) collective-permute-start(s32[1,8]{1,0:T(1,128)} %param.19), channel_id=1, source_target_pairs={{8,0},{9,1},{10,2},{11,3},{12,4},{13,5},{14,6},{15,7},{0,8},{1,9},... | collective-permute-start | bytes 104 | tf_op jit(solution)/shard_map/ppermute | solution.py:232
  4.1 5.6 %copy-start.1 = (bf16[12,32,128]{2,1,0:T(8,128)(2,1)S(1)}, bf16[12,32,128]{2,1,0:T(8,128)(2,1)}, u32[]{:S(2)}) copy-start(bf16[12,32,128]{2,1,0:T(8,128)(2,1)} %coarse_ref.1) | copy-start | bytes 294916
  5.8 16.0 %collective-permute-start.3 = (bf16[17,16,128]{2,1,0:T(8,128)(2,1)S(1)}, bf16[17,16,128]{2,1,0:T(8,128)(2,1)S(1)}, u32[]{:S(2)}, u32[]{:S(2)}) collective-permute-start(bf16[17,16,128]{2,1,0:T(8,128)(2,1)S(1)} %pad_maximum_fusion), channel_id=1, source_target_pairs={{6,0},{7,1},{8,2},{9,3},{10,4},{11,5},{12,6},{13,7},{14,8},{15,9},... | collective-permute-start | bytes 208904 | tf_op jit(solution)/shard_map/ppermute | solution.py:232
  9.7 8.9 %collective-permute-start.6 = (bf16[12,1,128]{2,1,0:T(2,128)(2,1)S(1)}, bf16[12,1,128]{2,1,0:T(2,128)(2,1)S(1)}, u32[]{:S(2)}, u32[]{:S(2)}) collective-permute-start(bf16[12,1,128]{2,1,0:T(2,128)(2,1)S(1)} %broadcast_select_fusion.2), channel_id=1, source_target_pairs={{0,1},{1,2},{2,3},{3,4},{4,5},{5,6},{6,7},{7,8},{8,9},{9,10},{10,1... | collective-permute-start | bytes 9224 | tf_op jit(solution)/shard_map/ppermute | solution.py:250
  11.0 20.5 %collective-permute-start.5 = (bf16[16,16,128]{2,1,0:T(8,128)(2,1)S(1)}, bf16[16,16,128]{2,1,0:T(8,128)(2,1)S(1)}, u32[]{:S(2)}, u32[]{:S(2)}) collective-permute-start(bf16[16,16,128]{2,1,0:T(8,128)(2,1)S(1)} %bitcast.42), channel_id=1, source_target_pairs={{8,0},{9,1},{10,2},{11,3},{12,4},{13,5},{14,6},{15,7},{0,8},{1,9},... | collective-permute-start | bytes 196616 | tf_op jit(solution)/shard_map/ppermute | solution.py:232
  12.0 0.7 %copy-start.8 = (bf16[128,8]{0,1:T(8,128)(2,1)S(1)}, bf16[128,8]{0,1:T(8,128)(2,1)}, u32[]{:S(2)}) copy-start(bf16[128,8]{0,1:T(8,128)(2,1)} %param.14) | copy-start | bytes 6148
  12.7 0.7 %copy-start.7 = (bf16[128,12]{0,1:T(8,128)(2,1)S(1)}, bf16[128,12]{0,1:T(8,128)(2,1)}, u32[]{:S(2)}) copy-start(bf16[128,12]{0,1:T(8,128)(2,1)} %param.11) | copy-start | bytes 9220
  13.4 5.2 %copy-start.5 = (bf16[4,128]{1,0:T(4,128)(2,1)S(1)}, bf16[4,128]{1,0:T(4,128)(2,1)}, u32[]{:S(2)}) copy-start(bf16[4,128]{1,0:T(4,128)(2,1)} %out_ref.3) | copy-start | bytes 3076
  13.5 8.3 %collective-permute-start.2 = (bf16[17,16,128]{2,1,0:T(8,128)(2,1)S(1)}, bf16[17,16,128]{2,1,0:T(8,128)(2,1)S(1)}, u32[]{:S(2)}, u32[]{:S(2)}) collective-permute-start(bf16[17,16,128]{2,1,0:T(8,128)(2,1)S(1)} %pad_maximum_fusion), channel_id=1, source_target_pairs={{4,0},{5,1},{6,2},{7,3},{8,4},{9,5},{10,6},{11,7},{12,8},{13,9},{1... | collective-permute-start | bytes 208904 | tf_op jit(solution)/shard_map/ppermute | solution.py:232
  17.2 4.7 %collective-permute-start.1 = (bf16[17,16,128]{2,1,0:T(8,128)(2,1)S(1)}, bf16[17,16,128]{2,1,0:T(8,128)(2,1)S(1)}, u32[]{:S(2)}, u32[]{:S(2)}) collective-permute-start(bf16[17,16,128]{2,1,0:T(8,128)(2,1)S(1)} %pad_maximum_fusion), channel_id=1, source_target_pairs={{2,0},{3,1},{4,2},{5,3},{6,4},{7,5},{8,6},{9,7},{10,8},{11,9},{12,... | collective-permute-start | bytes 208904 | tf_op jit(solution)/shard_map/ppermute | solution.py:232
  18.6 1.0 %copy-start.2 = (bf16[3,3,128,128]{3,2,1,0:T(8,128)(2,1)S(1)}, bf16[3,3,128,128]{3,2,1,0:T(8,128)(2,1)}, u32[]{:S(2)}) copy-start(bf16[3,3,128,128]{3,2,1,0:T(8,128)(2,1)} %conv_ref.1) | copy-start | bytes 884740
  19.5 2.5 %copy-start.3 = (bf16[4,4,32,128]{3,2,1,0:T(8,128)(2,1)S(1)}, bf16[4,4,32,128]{3,2,1,0:T(8,128)(2,1)}, u32[]{:S(2)}) copy-start(bf16[4,4,32,128]{3,2,1,0:T(8,128)(2,1)} %noise_ref.1) | copy-start | bytes 393220
  20.9 1.1 %copy-start.4 = (bf16[128,128]{1,0:T(8,128)(2,1)S(1)}, bf16[128,128]{1,0:T(8,128)(2,1)}, u32[]{:S(2)}) copy-start(bf16[128,128]{1,0:T(8,128)(2,1)} %mid_ref.3) | copy-start | bytes 98308
  20.9 10.6 %collective-permute-start.7 = (bf16[4,2048]{1,0:T(4,128)(2,1)S(1)}, bf16[4,2048]{1,0:T(4,128)(2,1)S(1)}, u32[]{:S(2)}, u32[]{:S(2)}) collective-permute-start(bf16[4,2048]{1,0:T(4,128)(2,1)S(1)} %regression.1.condition_ref.mine_ref), channel_id=1, source_target_pairs={{0,1},{1,0},{2,3},{3,2},{4,5},{5,4},{6,7},{7,6},{8,9},{9,8},{10,11... | collective-permute-start | bytes 49160 | tf_op jit(solution)/shard_map/ppermute | solution.py:237
  21.9 0.7 %copy-start.6 = (bf16[4,128]{1,0:T(4,128)(2,1)S(1)}, bf16[4,128]{1,0:T(4,128)(2,1)}, u32[]{:S(2)}) copy-start(bf16[4,128]{1,0:T(4,128)(2,1)} %out_ref.5) | copy-start | bytes 3076
  21.9 9.2 %collective-permute-start.4 = (s32[9,8]{1,0:T(8,128)S(1)}, s32[9,8]{1,0:T(8,128)S(1)}, u32[]{:S(2)}, u32[]{:S(2)}) collective-permute-start(s32[9,8]{1,0:T(8,128)S(1)} %stack.12), channel_id=1, source_target_pairs={{0,1},{1,0},{2,3},{3,2},{4,5},{5,4},{6,7},{7,6},{8,9},{9,8},{10,11... | collective-permute-start | bytes 872 | tf_op jit(solution)/shard_map/ppermute | solution.py:237
  41.8 1.3 %collective-permute-start.8 = (f32[2,4,16,128]{3,2,1,0:T(8,128)S(1)}, f32[2,4,16,128]{3,2,1,0:T(8,128)S(1)}, u32[]{:S(2)}, u32[]{:S(2)}) collective-permute-start(f32[2,4,16,128]{3,2,1,0:T(8,128)S(1)} %get-tuple-element.8), channel_id=1, source_target_pairs={{0,1},{1,0},{2,3},{3,2},{4,5},{5,4},{6,7},{7,6},{8,9},{9,8},{10,11... | collective-permute-start | bytes 196616 | tf_op jit(solution)/shard_map/ppermute | solution.py:237
  43.2 4.0 %collective-permute-start.9 = (f32[4,16,128]{2,1,0:T(8,128)S(1)}, f32[4,16,128]{2,1,0:T(8,128)S(1)}, u32[]{:S(2)}, u32[]{:S(2)}) collective-permute-start(f32[4,16,128]{2,1,0:T(8,128)S(1)} %fusion.1), channel_id=1, source_target_pairs={{0,16},{16,0},{1,17},{17,1},{2,18},{18,2},{3,19},{19,3},{4,20},{20... | collective-permute-start | bytes 98312 | tf_op jit(solution)/shard_map/ppermute | solution.py:241
where the time goes:
time: 48.1 us; the launch traced here: 47.8 us
  Pallas kernels  20.3 us (42%)
  starting transfers between devices  17.5 us (36%)
  waiting for transfers between devices  5.67 us (12%)
  local copies, waits for them, and re-layouts  3.44 us (7%)
  other arithmetic  0.74 us (2%)
    ppermute x5, starting transfers between devices, from_ahead(): lax.ppermute(block, 'tile', [((i + distance) % count, i) for i in range(c...  14 us
    pallas_call x1, Pallas kernels, body(): pl.pallas_call(slot_kernel, out_shape=(moments, moments), in_specs=[pl.Bl...  10.3 us
    pallas_call x1, Pallas kernels, body(): pl.pallas_call(base_kernel, out_shape=jax.ShapeDtypeStruct((2, channels,...  8.58 us
    unnamed x22, local copies, waits for them, and re-layouts  3.03 us
    ppermute x1, waiting for transfers between devices, swap_sections(): return lax.ppermute(block, 'section', [(0, 1), (1, 0)])  2.8 us
    ppermute x5, waiting for transfers between devices, from_ahead(): lax.ppermute(block, 'tile', [((i + distance) % count, i) for i in range(c...  1.65 us
    pallas_call x1, Pallas kernels, body(): pl.pallas_call(regress_kernel, out_shape=jax.ShapeDtypeStruct((channels,...  1.41 us
    ppermute x1, starting transfers between devices, edge_rows(): lax.ppermute(jnp.where(section == 0, last, first), ('section', 'tile'), p...  1.29 us
  transfers between devices with their start and end apart: 10, of which 3 were waited for; matrix products, arithmetic and copies ran while one was open for 1% of the time, Pallas kernels for 21%

commit v1 on v0

--- a/solution.py
+++ b/solution.py
@@ -47,6 +47,12 @@
     return jnp.dot(left, right, preferred_element_type=jnp.float32)
 
 
+def dot_rows(left, right):
+    return lax.dot_general(
+        left, right, (((0,), (0,)), ((), ())), preferred_element_type=jnp.float32
+    )
+
+
 def halved(weight):
     return (0.5 * weight.astype(jnp.float32)).astype(jnp.bfloat16)
 
@@ -56,7 +62,7 @@
     latent = start * noise
     for scale, keep, gain in steps:
         stacked = jnp.concatenate([(scale * latent).astype(jnp.bfloat16), condition], axis=0)
-        hidden = half_silu(dot(w_in, stacked))
+        hidden = half_silu(dot_rows(w_in, stacked))
         hidden = half_silu(dot(w_mid, hidden))
         latent = keep * latent + gain * dot(w_out, hidden)
     return condition.astype(jnp.float32) + latent
@@ -66,17 +72,43 @@
     return field.astype(jnp.float32).reshape(field.shape[0], -1)
 
 
-def regress_kernel(coarse_ref, edge_ref, lift_ref, conv_ref, out_ref, condition_ref):
+def regress_kernel(
+    coarse_ref,
+    edge_ref,
+    lift_hbm,
+    conv_hbm,
+    out_hbm,
+    in_hbm,
+    mid_hbm,
+    condition_ref,
+    in_ref,
+    mid_ref,
+    lift_ref,
+    conv_ref,
+    out_ref,
+    sems,
+):
     section = lax.axis_index("section")
     channels_in, rows_all, width = coarse_ref.shape
     rows = rows_all // SECTIONS
+    pairs = (
+        (lift_hbm, lift_ref),
+        (conv_hbm, conv_ref),
+        (out_hbm, out_ref),
+        (in_hbm, in_ref),
+        (mid_hbm, mid_ref),
+    )
+    copies = [pltpu.make_async_copy(a, b, sems.at[i]) for i, (a, b) in enumerate(pairs)]
+    for copy in copies:
+        copy.start()
     coarse = coarse_ref[...].astype(jnp.float32)
     edge = edge_ref[...].astype(jnp.float32)
     upper = jnp.concatenate([edge, coarse[:, : rows + 1]], axis=1)
     lower = jnp.concatenate([coarse[:, rows - 1 :], edge], axis=1)
     window = jnp.where(section == 0, upper, lower)
     window = window.reshape(channels_in, (rows + 2) * width).astype(jnp.bfloat16)
-    half = dot(halved(lift_ref[...]), window)
+    copies[0].wait()
+    half = dot_rows(halved(lift_ref[...]), window)
     lifted = half * jnp.tanh(half) + half
     channels = lifted.shape[0]
     column = lax.broadcasted_iota(jnp.int32, (channels, width), 1)
@@ -87,17 +119,17 @@
         right = jnp.where(column == width - 1, 0.0, pltpu.roll(piece, width - 1, 1))
         taps.append(jnp.concatenate([left, piece, right], axis=0).astype(jnp.bfloat16))
     stacked = jnp.concatenate(taps, axis=1)
+    copies[1].wait()
     half = None
     for tap in range(3):
         weight = halved(conv_ref[tap].reshape(3 * channels, channels))
-        part = lax.dot_general(
-            weight,
-            stacked[:, tap * width : (tap + rows) * width],
-            (((0,), (0,)), ((), ())),
-            preferred_element_type=jnp.float32,
-        )
+        part = dot_rows(weight, stacked[:, tap * width : (tap + rows) * width])
         half = part if half is None else half + part
+    for copy in copies[2:]:
+        copy.wait()
     condition_ref[...] = dot(out_ref[...], half_silu(half)).astype(jnp.bfloat16)
+    in_ref[...] = halved(in_ref[...])
+    mid_ref[...] = halved(mid_ref[...])
 
 
 def base_kernel(noise_ref, condition_ref, in_ref, mid_ref, out_ref, sums_ref):
@@ -113,8 +145,8 @@
     samples = denoise(
         jnp.concatenate(noise, axis=1),
         jnp.concatenate([condition] * members, axis=1),
-        halved(in_ref[...]),
-        halved(mid_ref[...]),
+        in_ref[...],
+        mid_ref[...],
         out_ref[...],
     )
     cells = rows * width
@@ -196,27 +228,33 @@
     peer_scale = 1.0 / members_of(peer_row).astype(jnp.float32)
     sample_ref[0] = base_ref[...]
     sample_ref[1] = jnp.zeros_like(base_ref)
-    w_in, w_mid, w_out = halved(in_ref[...]), halved(mid_ref[...]), out_ref[...]
-    group = 2
-
-    @pl.loop(0, (count + group - 1) // group)
-    def _(turn):
+    w_in, w_mid, w_out = in_ref[...], mid_ref[...], out_ref[...]
+
+    def run(first, group):
         noise, conditions, sides = [], [], []
         for member in range(group):
-            place = group * turn + member
-            side = where_ref[jnp.minimum(place, count - 1)]
+            side = where_ref[jnp.minimum(first + member, count - 1)]
             sides.append(side)
-            noise.append(flat(noise_ref[place]))
+            noise.append(flat(noise_ref[first + member]))
             conditions.append(jnp.where(side == 0, mine_ref[...], theirs_ref[...]))
         samples = denoise(
             jnp.concatenate(noise, axis=1), jnp.concatenate(conditions, axis=1), w_in, w_mid, w_out
         )
         for member in range(group):
-            live = group * turn + member < count
             sample = samples[:, member * cells : (member + 1) * cells]
-            sample = jnp.where(live, sample, 0.0)
+            sample = jnp.where(first + member < count, sample, 0.0)
             sample_ref[sides[member], 0] += sample
             sample_ref[sides[member], 1] += sample * sample
+
+    fours = (count + 1) // 4
+
+    @pl.loop(0, fours)
+    def _(turn):
+        run(4 * turn, 4)
+
+    @pl.when(count > 4 * fours)
+    def _():
+        run(4 * fours, 2)
 
     for moment in range(2):
         own_ref[moment] = (own_scale * sample_ref[0, moment]).reshape(channels, rows, width)
@@ -276,14 +314,29 @@
     edge = edge_rows(coarse, section)
     half_noise = lax.dynamic_slice_in_dim(slot_noise, rows * section, rows, axis=2)
     half_noise = half_noise.reshape(slots * channels, rows, width)
-    far8_noise = from_ahead(half_noise, 8)
-    far8_routes = from_ahead(extra_dest, 8)
-
-    condition = pl.pallas_call(
+
+    def record_of(routes):
+        block = jnp.pad(routes.astype(jnp.bfloat16), ((0, rows - routes.shape[0]), (0, width - REACH)))
+        return jnp.concatenate([half_noise, block[None]], axis=0)
+
+    far8 = from_ahead(record_of(extra_dest), 8)
+
+    weight = jax.ShapeDtypeStruct((2 * channels, hidden), jnp.bfloat16)
+    condition, w_in, w_mid = pl.pallas_call(
         regress_kernel,
-        out_shape=jax.ShapeDtypeStruct((channels, cells), jnp.bfloat16),
-        in_specs=in_vmem(5),
-        out_specs=pl.BlockSpec(memory_space=pltpu.VMEM),
+        out_shape=(
+            jax.ShapeDtypeStruct((channels, cells), jnp.bfloat16),
+            weight,
+            jax.ShapeDtypeStruct((hidden, hidden), jnp.bfloat16),
+        ),
+        in_specs=in_vmem(2) + [pl.BlockSpec(memory_space=pl.ANY)] * 5,
+        out_specs=(pl.BlockSpec(memory_space=pltpu.VMEM),) * 3,
+        scratch_shapes=[
+            pltpu.VMEM((coarse.shape[0], hidden), jnp.bfloat16),
+            pltpu.VMEM(conv_weight.shape, jnp.bfloat16),
+            pltpu.VMEM(out_weight.shape, jnp.bfloat16),
+            pltpu.SemaphoreType.DMA((5,)),
+        ],
         compiler_params=params,
         cost_estimate=pl.CostEstimate(
             flops=2 * cells * hidden * (9 * hidden + 16),
@@ -291,11 +344,11 @@
             transcendentals=2 * cells * hidden,
         ),
         name="regression",
-    )(coarse, edge, lift_weight, conv_weight, out_weight)
-
-    pair = jnp.concatenate([extra_dest, far8_routes], axis=0).astype(jnp.bfloat16)
-    pair = jnp.pad(pair, ((0, rows - 2), (0, width - REACH)))
-    record = jnp.concatenate([half_noise, pair[None]], axis=0)
+    )(coarse, edge, lift_weight.T, conv_weight, out_weight, denoise_in.T, denoise_mid)
+
+    far8_after, condition = lax.optimization_barrier((far8, condition))
+    far8_routes = far8_after[-1, :1, :REACH].astype(jnp.int32)
+    record = record_of(jnp.concatenate([extra_dest, far8_routes], axis=0))
     far2, far4, far6 = [from_ahead(record, distance) for distance in (2, 4, 6)]
     got = [r[-1, :2, :REACH].astype(jnp.int32) for r in (far2, far4, far6)]
     if count == 2 * REACH:
@@ -322,7 +375,7 @@
             transcendentals=2 * NSTEP * members * cells * hidden,
         ),
         name="base_members",
-    )(base_noise, condition, denoise_in, denoise_mid, denoise_out)
+    )(base_noise, condition, w_in, w_mid, denoise_out)
 
     moments = jax.ShapeDtypeStruct((2, channels, rows, width), jnp.float32)
     own, peer = pl.pallas_call(
@@ -331,9 +384,9 @@
         in_specs=[pl.BlockSpec(memory_space=pltpu.SMEM)] + in_vmem(11),
         out_specs=(pl.BlockSpec(memory_space=pltpu.VMEM),) * 2,
         scratch_shapes=[
-            pltpu.VMEM((2 * 5, channels, rows, width), jnp.bfloat16),
+            pltpu.VMEM((12, channels, rows, width), jnp.bfloat16),
             pltpu.VMEM((2, 2, channels, cells), jnp.float32),
-            pltpu.SMEM((2 * 5,), jnp.int32),
+            pltpu.SMEM((12,), jnp.int32),
         ],
         compiler_params=params,
         cost_estimate=pl.CostEstimate(
@@ -348,12 +401,12 @@
         far2,
         far4,
         far6,
-        far8_noise,
+        far8,
         condition,
         peer_condition,
         base,
-        denoise_in,
-        denoise_mid,
+        w_in,
+        w_mid,
         denoise_out,
     )
     total = own + swap_cores(peer)

time: 48.1 us -> 49.7 us (1.033)
  waiting for transfers between devices: 5.67 us -> 8.29 us
  starting transfers between devices: 17.5 us -> 15.5 us
  Pallas kernels: 20.3 us -> 21.1 us
    ppermute x5 -> x4, waiting for transfers between devices: 1.65 us -> 2.88 us  [from_ahead(): lax.ppermute(block, 'tile', [((i + distance) % count, i) for i in range(c...]
    ppermute x1, starting transfers between devices: 1.18 us -> 0.28 us  [swap_sections(): return lax.ppermute(block, 'section', [(0, 1), (1, 0)])]
    ppermute x1, waiting for transfers between devices: 2.8 us -> 3.7 us  [swap_sections(): return lax.ppermute(block, 'section', [(0, 1), (1, 0)])]
    ppermute x5 -> x4, starting transfers between devices: 14 us -> 13.1 us  [from_ahead(): lax.ppermute(block, 'tile', [((i + distance) % count, i) for i in range(c...]
    ppermute x1, waiting for transfers between devices: 0.01 us -> 0.81 us  [edge_rows(): lax.ppermute(jnp.where(section == 0, last, first), ('section', 'tile'), p...]
    pallas_call x1, Pallas kernels: 1.41 us -> 2.11 us  [body(): pl.pallas_call(regress_kernel, out_shape=(jax.ShapeDtypeStruct((channels,...]
    unnamed x22 -> x20, local copies, waits for them, and re-layouts: 3.03 us -> 3.22 us
  transfers between devices with their start and end apart: 10 -> 9, of which waited for: 3 -> 5; matrix products, arithmetic and copies ran while one was open for 1% -> 1% of each run, Pallas kernels for 21% -> 22%
where the time goes in v1:
time: 49.7 us; the launch traced here: 49.4 us
  Pallas kernels  21.1 us (42%)
  starting transfers between devices  15.5 us (31%)
  waiting for transfers between devices  8.29 us (17%)
  local copies, waits for them, and re-layouts  3.64 us (7%)
  other arithmetic  0.75 us (2%)
    ppermute x4, starting transfers between devices, from_ahead(): lax.ppermute(block, 'tile', [((i + distance) % count, i) for i in range(c...  13.1 us
    pallas_call x1, Pallas kernels, body(): pl.pallas_call(slot_kernel, out_shape=(moments, moments), in_specs=[pl.Bl...  10.3 us
    pallas_call x1, Pallas kernels, body(): pl.pallas_call(base_kernel, out_shape=jax.ShapeDtypeStruct((2, channels,...  8.7 us
    ppermute x1, waiting for transfers between devices, swap_sections(): return lax.ppermute(block, 'section', [(0, 1), (1, 0)])  3.7 us
    unnamed x20, local copies, waits for them, and re-layouts  3.22 us
    ppermute x4, waiting for transfers between devices, from_ahead(): lax.ppermute(block, 'tile', [((i + distance) % count, i) for i in range(c...  2.88 us
    pallas_call x1, Pallas kernels, body(): pl.pallas_call(regress_kernel, out_shape=(jax.ShapeDtypeStruct((channels,...  2.11 us
    ppermute x1, starting transfers between devices, edge_rows(): lax.ppermute(jnp.where(section == 0, last, first), ('section', 'tile'), p...  1.46 us
  transfers between devices with their start and end apart: 9, of which 5 were waited for; matrix products, arithmetic and copies ran while one was open for 1% of the time, Pallas kernels for 22%

profile of v1, /device:TPU:0, one launch (start us, length us, event | category | flops | bytes accessed | tf_op | source)
XLA Modules:
  0.0 49.4 jit_solution(5059415035350258780)
XLA Ops:
  0.0 0.0 copy-start
  0.0 0.0 copy-start.9
  0.0 0.7 %copy-done.9 = s32[1,8]{1,0:T(1,128)S(1)} copy-done((s32[1,8]{1,0:T(1,128)S(1)}, s32[1,8]{1,0:T(1,128)}, u32[]{:S(2)}) %copy-start.9) | copy-done | bytes 56
  0.7 0.2 copy-done
  0.9 0.0 copy-start.1
  0.9 0.0 copy-start.4
  1.0 4.1 %collective-permute-start = (bf16[17,16,128]{2,1,0:T(8,128)(2,1)S(1)}, bf16[17,16,128]{2,1,0:T(8,128)(2,1)S(1)}, u32[]{:S(2)}, u32[]{:S(2)}) collective-permute-start(bf16[17,16,128]{2,1,0:T(8,128)(2,1)S(1)} %pad_maximum_fusion), channel_id=1, source_target_pairs={{8,0},{9,1},{10,2},{11,3},{12,4},{13,5},{14,6},{15,7},{0,8},{1,9},... | collective-permute-start | bytes 208904 | tf_op jit(solution)/shard_map/ppermute | solution.py:270
  5.1 0.0 copy-done.1
  5.1 0.0 copy-start.5
  5.1 0.0 copy-start.6
  5.1 1.5 %collective-permute-start.1 = (bf16[12,1,128]{2,1,0:T(2,128)(2,1)S(1)}, bf16[12,1,128]{2,1,0:T(2,128)(2,1)S(1)}, u32[]{:S(2)}, u32[]{:S(2)}) collective-permute-start(bf16[12,1,128]{2,1,0:T(2,128)(2,1)S(1)} %broadcast_select_fusion.2), channel_id=1, source_target_pairs={{0,1},{1,2},{2,3},{3,4},{4,5},{5,6},{6,7},{7,8},{8,9},{9,10},{10,1... | collective-permute-start | bytes 9224 | tf_op jit(solution)/shard_map/ppermute | solution.py:288
  6.6 0.8 %collective-permute-done.1.edge_ref = bf16[12,1,128]{2,1,0:T(2,128)(2,1)S(1)} collective-permute-done((bf16[12,1,128]{2,1,0:T(2,128)(2,1)S(1)}, bf16[12,1,128]{2,1,0:T(2,128)(2,1)S(1)}, u32[]{:S(2)}, u32[]{:S(2)}) %collective-permute-start.1) | collective-permute-done | bytes 3104 | tf_op jit(solution)/shard_map/ppermute | solution.py:288
  7.4 0.0 copy-start.7
  7.4 0.0 copy-done.4
  7.4 0.0 copy-done.5
  7.4 0.0 copy-done.6
  7.4 0.7 %copy-done.7 = bf16[4,128]{1,0:T(4,128)(2,1)S(1)} copy-done((bf16[4,128]{1,0:T(4,128)(2,1)S(1)}, bf16[4,128]{1,0:T(4,128)(2,1)}, u32[]{:S(2)}) %copy-start.7) | copy-done | bytes 1048
  8.0 0.0 copy-start.2
  8.0 1.0 %copy-done.2 = bf16[3,3,128,128]{3,2,1,0:T(8,128)(2,1)S(1)} copy-done((bf16[3,3,128,128]{3,2,1,0:T(8,128)(2,1)S(1)}, bf16[3,3,128,128]{3,2,1,0:T(8,128)(2,1)}, u32[]{:S(2)}) %copy-start.2) | copy-done | bytes 294936
  9.0 2.1 %regression.1 = (bf16[4,2048]{1,0:T(4,128)(2,1)S(1)}, bf16[8,128]{1,0:T(8,128)(2,1)S(1)}, bf16[128,128]{1,0:T(8,128)(2,1)S(1)}) custom-call(bf16[12,32,128]{2,1,0:T(8,128)(2,1)S(1)} %copy-done.1, bf16[12,1,128]{2,1,0:T(2,128)(2,1)S(1)} %collective-permute-done.1.edge_ref, bf16[12,128]{1,0:T(8,128)(2,1)S(1)} %bitcast.53, ...), custom_call_target="tpu_custom_call" | custom-call | flops 612368384 | bytes 600000 | tf_op jit(solution)/shard_map/regression/pallas_call | solution.py:325
  11.1 0.0 copy-start.3
  11.1 0.0 collective-permute-done.far8_ref
  11.2 4.5 %collective-permute-start.4 = (bf16[17,16,128]{2,1,0:T(8,128)(2,1)S(1)}, bf16[17,16,128]{2,1,0:T(8,128)(2,1)S(1)}, u32[]{:S(2)}, u32[]{:S(2)}) collective-permute-start(bf16[17,16,128]{2,1,0:T(8,128)(2,1)S(1)} %pad_maximum_fusion.1), channel_id=1, source_target_pairs={{6,0},{7,1},{8,2},{9,3},{10,4},{11,5},{12,6},{13,7},{14,8},{15,9},... | collective-permute-start | bytes 208904 | tf_op jit(solution)/shard_map/ppermute | solution.py:270
  15.7 3.1 %collective-permute-start.3 = (bf16[17,16,128]{2,1,0:T(8,128)(2,1)S(1)}, bf16[17,16,128]{2,1,0:T(8,128)(2,1)S(1)}, u32[]{:S(2)}, u32[]{:S(2)}) collective-permute-start(bf16[17,16,128]{2,1,0:T(8,128)(2,1)S(1)} %pad_maximum_fusion.1), channel_id=1, source_target_pairs={{4,0},{5,1},{6,2},{7,3},{8,4},{9,5},{10,6},{11,7},{12,8},{13,9},{1... | collective-permute-start | bytes 208904 | tf_op jit(solution)/shard_map/ppermute | solution.py:270
  18.8 1.4 %collective-permute-start.2 = (bf16[17,16,128]{2,1,0:T(8,128)(2,1)S(1)}, bf16[17,16,128]{2,1,0:T(8,128)(2,1)S(1)}, u32[]{:S(2)}, u32[]{:S(2)}) collective-permute-start(bf16[17,16,128]{2,1,0:T(8,128)(2,1)S(1)} %pad_maximum_fusion.1), channel_id=1, source_target_pairs={{2,0},{3,1},{4,2},{5,3},{6,4},{7,5},{8,6},{9,7},{10,8},{11,9},{12,... | collective-permute-start | bytes 208904 | tf_op jit(solution)/shard_map/ppermute | solution.py:270
  20.2 0.0 collective-permute-start.6
  20.2 0.0 collective-permute-done.4.far6_ref
  20.2 0.8 %collective-permute-done.3.far4_ref = bf16[17,16,128]{2,1,0:T(8,128)(2,1)S(1)} collective-permute-done((bf16[17,16,128]{2,1,0:T(8,128)(2,1)S(1)}, bf16[17,16,128]{2,1,0:T(8,128)(2,1)S(1)}, u32[]{:S(2)}, u32[]{:S(2)}) %collective-permute-start.3) | collective-permute-done | bytes 69664 | tf_op jit(solution)/shard_map/ppermute | solution.py:270
  21.1 2.1 %collective-permute-done.2.far2_ref = bf16[17,16,128]{2,1,0:T(8,128)(2,1)S(1)} collective-permute-done((bf16[17,16,128]{2,1,0:T(8,128)(2,1)S(1)}, bf16[17,16,128]{2,1,0:T(8,128)(2,1)S(1)}, u32[]{:S(2)}, u32[]{:S(2)}) %collective-permute-start.2) | collective-permute-done | bytes 69664 | tf_op jit(solution)/shard_map/ppermute | solution.py:270
  23.2 0.1 collective-permute-start.5
  23.3 0.0 copy-start.8
  23.3 0.0 copy-done.3
  23.3 0.7 %copy-done.8 = bf16[4,128]{1,0:T(4,128)(2,1)S(1)} copy-done((bf16[4,128]{1,0:T(4,128)(2,1)S(1)}, bf16[4,128]{1,0:T(4,128)(2,1)}, u32[]{:S(2)}) %copy-start.8) | copy-done | bytes 1048
  23.9 8.7 %base_members.1.base_ref = f32[2,4,2048]{2,1,0:T(4,128)S(1)} custom-call(bf16[4,4,32,128]{3,2,1,0:T(8,128)(2,1)S(1)} %copy-done.3, bf16[4,2048]{1,0:T(4,128)(2,1)S(1)} %get-tuple-element.14.condition_ref.mine_ref, bf16[8,128]{1,0:T(8,128)(2,1)S(1)} %get-tuple-element.15.in_ref, bf16[128,128]{1,0:T(8,128)(2,1)S(1)} %get-tuple-element.16.mid_ref, ...), custom_call_target="tpu_custom_call" | custom-call | flops 1761607680 | bytes 400000 | tf_op jit(solution)/shard_map/base_members/pallas_call | solution.py:366
  32.6 0.0 collective-permute-done.5
  32.7 0.1 copy.13
  32.7 0.1 copy.14
  32.8 0.1 copy.15
  32.9 0.1 reshape.30.routes_ref
  33.0 0.0 collective-permute-done.6.theirs_ref
  33.0 10.3 %slot_members.1 = (f32[2,4,16,128]{3,2,1,0:T(8,128)S(1)}, f32[2,4,16,128]{3,2,1,0:T(8,128)S(1)}) custom-call(s32[144]{0:T(256)S(1)} %reshape.30.routes_ref, bf16[16,16,128]{2,1,0:T(8,128)(2,1)S(1)} %bitcast.52, bf16[17,16,128]{2,1,0:T(8,128)(2,1)S(1)} %collective-permute-done.2.far2_ref, bf16[17,16,128]{2,1,0:T(8,128)(2,1)S(1)} %collective-permute-done.3.far4_ref, ...), custom_call_target="tpu_custom_call" | custom-call | flops 1761607680 | bytes 1000000 | tf_op jit(solution)/shard_map/slot_members/pallas_call | solution.py:381
  43.3 0.6 %collective-permute-start.7 = (f32[2,4,16,128]{3,2,1,0:T(8,128)S(1)}, f32[2,4,16,128]{3,2,1,0:T(8,128)S(1)}, u32[]{:S(2)}, u32[]{:S(2)}) collective-permute-start(f32[2,4,16,128]{3,2,1,0:T(8,128)S(1)} %get-tuple-element.18), channel_id=1, source_target_pairs={{0,1},{1,0},{2,3},{3,2},{4,5},{5,4},{6,7},{7,6},{8,9},{9,8},{10,11... | collective-permute-start | bytes 196616 | tf_op jit(solution)/shard_map/ppermute | solution.py:275
  43.9 0.9 %collective-permute-done.7 = f32[2,4,16,128]{3,2,1,0:T(8,128)S(1)} collective-permute-done((f32[2,4,16,128]{3,2,1,0:T(8,128)S(1)}, f32[2,4,16,128]{3,2,1,0:T(8,128)S(1)}, u32[]{:S(2)}, u32[]{:S(2)}) %collective-permute-start.7) | collective-permute-done | bytes 65568 | tf_op jit(solution)/shard_map/ppermute | solution.py:275
  44.8 0.3 collective-permute-start.8
  45.1 3.7 %collective-permute-done.8 = f32[4,16,128]{2,1,0:T(8,128)S(1)} collective-permute-done((f32[4,16,128]{2,1,0:T(8,128)S(1)}, f32[4,16,128]{2,1,0:T(8,128)S(1)}, u32[]{:S(2)}, u32[]{:S(2)}) %collective-permute-start.8) | collective-permute-done | bytes 32800 | tf_op jit(solution)/shard_map/ppermute | solution.py:279
  48.8 0.6 %maximum_bitcast_fusion = f32[1,4,32,128]{3,2,1,0:T(8,128)} fusion(f32[4,16,128]{2,1,0:T(8,128)S(1)} %get-tuple-element.20, f32[4,16,128]{2,1,0:T(8,128)S(1)} %get-tuple-element.19), kind=kLoop, calls=%fused_computation.2 | loop fusion | flops 16384 | bytes 131072 | tf_op jit(solution)/shard_map/broadcast_in_dim | solution.py:420
  (20 shorter events, 0.2 us)
Async XLA Ops:
  0.0 0.9 %copy-start = (bf16[4,4,32,128]{3,2,1,0:T(8,128)(2,1)S(1)}, bf16[4,4,32,128]{3,2,1,0:T(8,128)(2,1)}, u32[]{:S(2)}) copy-start(bf16[4,4,32,128]{3,2,1,0:T(8,128)(2,1)} %param.18) | copy-start | bytes 393220
  0.0 0.7 %copy-start.9 = (s32[1,8]{1,0:T(1,128)S(1)}, s32[1,8]{1,0:T(1,128)}, u32[]{:S(2)}) copy-start(s32[1,8]{1,0:T(1,128)} %param.19) | copy-start | bytes 100
  0.9 4.1 %copy-start.1 = (bf16[12,32,128]{2,1,0:T(8,128)(2,1)S(1)}, bf16[12,32,128]{2,1,0:T(8,128)(2,1)}, u32[]{:S(2)}) copy-start(bf16[12,32,128]{2,1,0:T(8,128)(2,1)} %coarse_ref.1) | copy-start | bytes 294916
  0.9 6.4 %copy-start.4 = (bf16[128,128]{1,0:T(8,128)(2,1)S(1)}, bf16[128,128]{1,0:T(8,128)(2,1)}, u32[]{:S(2)}) copy-start(bf16[128,128]{1,0:T(8,128)(2,1)} %mid_hbm.1) | copy-start | bytes 98308
  1.0 10.2 %collective-permute-start = (bf16[17,16,128]{2,1,0:T(8,128)(2,1)S(1)}, bf16[17,16,128]{2,1,0:T(8,128)(2,1)S(1)}, u32[]{:S(2)}, u32[]{:S(2)}) collective-permute-start(bf16[17,16,128]{2,1,0:T(8,128)(2,1)S(1)} %pad_maximum_fusion), channel_id=1, source_target_pairs={{8,0},{9,1},{10,2},{11,3},{12,4},{13,5},{14,6},{15,7},{0,8},{1,9},... | collective-permute-start | bytes 208904 | tf_op jit(solution)/shard_map/ppermute | solution.py:270
  5.1 2.3 %copy-start.5 = (bf16[128,12]{0,1:T(8,128)(2,1)S(1)}, bf16[128,12]{0,1:T(8,128)(2,1)}, u32[]{:S(2)}) copy-start(bf16[128,12]{0,1:T(8,128)(2,1)} %param.11) | copy-start | bytes 9220
  5.1 2.3 %copy-start.6 = (bf16[128,8]{0,1:T(8,128)(2,1)S(1)}, bf16[128,8]{0,1:T(8,128)(2,1)}, u32[]{:S(2)}) copy-start(bf16[128,8]{0,1:T(8,128)(2,1)} %param.14) | copy-start | bytes 6148
  5.1 2.3 %collective-permute-start.1 = (bf16[12,1,128]{2,1,0:T(2,128)(2,1)S(1)}, bf16[12,1,128]{2,1,0:T(2,128)(2,1)S(1)}, u32[]{:S(2)}, u32[]{:S(2)}) collective-permute-start(bf16[12,1,128]{2,1,0:T(2,128)(2,1)S(1)} %broadcast_select_fusion.2), channel_id=1, source_target_pairs={{0,1},{1,2},{2,3},{3,4},{4,5},{5,6},{6,7},{7,8},{8,9},{9,10},{10,1... | collective-permute-start | bytes 9224 | tf_op jit(solution)/shard_map/ppermute | solution.py:288
  7.4 0.7 %copy-start.7 = (bf16[4,128]{1,0:T(4,128)(2,1)S(1)}, bf16[4,128]{1,0:T(4,128)(2,1)}, u32[]{:S(2)}) copy-start(bf16[4,128]{1,0:T(4,128)(2,1)} %out_hbm.1) | copy-start | bytes 3076
  8.0 1.0 %copy-start.2 = (bf16[3,3,128,128]{3,2,1,0:T(8,128)(2,1)S(1)}, bf16[3,3,128,128]{3,2,1,0:T(8,128)(2,1)}, u32[]{:S(2)}) copy-start(bf16[3,3,128,128]{3,2,1,0:T(8,128)(2,1)} %conv_hbm.1) | copy-start | bytes 884740
  11.1 12.1 %copy-start.3 = (bf16[4,4,32,128]{3,2,1,0:T(8,128)(2,1)S(1)}, bf16[4,4,32,128]{3,2,1,0:T(8,128)(2,1)}, u32[]{:S(2)}) copy-start(bf16[4,4,32,128]{3,2,1,0:T(8,128)(2,1)} %noise_ref.1) | copy-start | bytes 393220
  11.2 9.0 %collective-permute-start.4 = (bf16[17,16,128]{2,1,0:T(8,128)(2,1)S(1)}, bf16[17,16,128]{2,1,0:T(8,128)(2,1)S(1)}, u32[]{:S(2)}, u32[]{:S(2)}) collective-permute-start(bf16[17,16,128]{2,1,0:T(8,128)(2,1)S(1)} %pad_maximum_fusion.1), channel_id=1, source_target_pairs={{6,0},{7,1},{8,2},{9,3},{10,4},{11,5},{12,6},{13,7},{14,8},{15,9},... | collective-permute-start | bytes 208904 | tf_op jit(solution)/shard_map/ppermute | solution.py:270
  15.7 5.4 %collective-permute-start.3 = (bf16[17,16,128]{2,1,0:T(8,128)(2,1)S(1)}, bf16[17,16,128]{2,1,0:T(8,128)(2,1)S(1)}, u32[]{:S(2)}, u32[]{:S(2)}) collective-permute-start(bf16[17,16,128]{2,1,0:T(8,128)(2,1)S(1)} %pad_maximum_fusion.1), channel_id=1, source_target_pairs={{4,0},{5,1},{6,2},{7,3},{8,4},{9,5},{10,6},{11,7},{12,8},{13,9},{1... | collective-permute-start | bytes 208904 | tf_op jit(solution)/shard_map/ppermute | solution.py:270
  18.8 4.3 %collective-permute-start.2 = (bf16[17,16,128]{2,1,0:T(8,128)(2,1)S(1)}, bf16[17,16,128]{2,1,0:T(8,128)(2,1)S(1)}, u32[]{:S(2)}, u32[]{:S(2)}) collective-permute-start(bf16[17,16,128]{2,1,0:T(8,128)(2,1)S(1)} %pad_maximum_fusion.1), channel_id=1, source_target_pairs={{2,0},{3,1},{4,2},{5,3},{6,4},{7,5},{8,6},{9,7},{10,8},{11,9},{12,... | collective-permute-start | bytes 208904 | tf_op jit(solution)/shard_map/ppermute | solution.py:270
  20.2 12.8 %collective-permute-start.6 = (bf16[4,2048]{1,0:T(4,128)(2,1)S(1)}, bf16[4,2048]{1,0:T(4,128)(2,1)S(1)}, u32[]{:S(2)}, u32[]{:S(2)}) collective-permute-start(bf16[4,2048]{1,0:T(4,128)(2,1)S(1)} %get-tuple-element.14.condition_ref.mine_ref), channel_id=1, source_target_pairs={{0,1},{1,0},{2,3},{3,2},{4,5},{5,4},{6,7},{7,6},{8,9},{9,8},{10,11... | collective-permute-start | bytes 49160 | tf_op jit(solution)/shard_map/ppermute | solution.py:275
  23.2 9.5 %collective-permute-start.5 = (s32[9,8]{1,0:T(8,128)S(1)}, s32[9,8]{1,0:T(8,128)S(1)}, u32[]{:S(2)}, u32[]{:S(2)}) collective-permute-start(s32[9,8]{1,0:T(8,128)S(1)} %stack.12), channel_id=1, source_target_pairs={{0,1},{1,0},{2,3},{3,2},{4,5},{5,4},{6,7},{7,6},{8,9},{9,8},{10,11... | collective-permute-start | bytes 872 | tf_op jit(solution)/shard_map/ppermute | solution.py:275
  23.3 0.7 %copy-start.8 = (bf16[4,128]{1,0:T(4,128)(2,1)S(1)}, bf16[4,128]{1,0:T(4,128)(2,1)}, u32[]{:S(2)}) copy-start(bf16[4,128]{1,0:T(4,128)(2,1)} %out_ref.3) | copy-start | bytes 3076
  43.3 1.5 %collective-permute-start.7 = (f32[2,4,16,128]{3,2,1,0:T(8,128)S(1)}, f32[2,4,16,128]{3,2,1,0:T(8,128)S(1)}, u32[]{:S(2)}, u32[]{:S(2)}) collective-permute-start(f32[2,4,16,128]{3,2,1,0:T(8,128)S(1)} %get-tuple-element.18), channel_id=1, source_target_pairs={{0,1},{1,0},{2,3},{3,2},{4,5},{5,4},{6,7},{7,6},{8,9},{9,8},{10,11... | collective-permute-start | bytes 196616 | tf_op jit(solution)/shard_map/ppermute | solution.py:275
  44.8 4.0 %collective-permute-start.8 = (f32[4,16,128]{2,1,0:T(8,128)S(1)}, f32[4,16,128]{2,1,0:T(8,128)S(1)}, u32[]{:S(2)}, u32[]{:S(2)}) collective-permute-start(f32[4,16,128]{2,1,0:T(8,128)S(1)} %fusion.1), channel_id=1, source_target_pairs={{0,16},{16,0},{1,17},{17,1},{2,18},{18,2},{3,19},{19,3},{4,20},{20... | collective-permute-start | bytes 98312 | tf_op jit(solution)/shard_map/ppermute | solution.py:279

commit v2 on v1

--- a/solution.py
+++ b/solution.py
@@ -80,9 +80,11 @@
     out_hbm,
     in_hbm,
     mid_hbm,
+    last_hbm,
     condition_ref,
     in_ref,
     mid_ref,
+    last_ref,
     lift_ref,
     conv_ref,
     out_ref,
@@ -97,6 +99,7 @@
         (out_hbm, out_ref),
         (in_hbm, in_ref),
         (mid_hbm, mid_ref),
+        (last_hbm, last_ref),
     )
     copies = [pltpu.make_async_copy(a, b, sems.at[i]) for i, (a, b) in enumerate(pairs)]
     for copy in copies:
@@ -155,77 +158,92 @@
     sums_ref[1] = functools.reduce(lambda a, b: a + b, [p * p for p in pieces])
 
 
-def slot_kernel(
-    routes_ref,
-    near_ref,
-    far2_ref,
-    far4_ref,
-    far6_ref,
-    far8_ref,
-    mine_ref,
-    theirs_ref,
-    base_ref,
-    in_ref,
-    mid_ref,
-    out_ref,
-    own_ref,
-    peer_ref,
-    noise_ref,
-    sample_ref,
-    where_ref,
-):
-    tile = lax.axis_index("tile")
-    tiles = lax.axis_size("tile")
+def slot_plan(table, tile, tiles):
     core = lax.rem(tile, 2)
-    chip_tile = tile - core
+    chip = lax.broadcasted_iota(jnp.int32, table.shape, 0)
+    lane = lax.broadcasted_iota(jnp.int32, table.shape, 1)
+    device = REACH + core + 2 * lane
+    known = chip < 9
+    parity = []
+    for odd in range(2):
+        index = 2 * chip + odd
+        ids = tile - core + index - REACH
+        ids = jnp.where(ids < 0, ids + tiles, ids)
+        ids = jnp.where(ids >= tiles, ids - tiles, ids)
+        part = table[:, odd * REACH : (odd + 1) * REACH]
+        named = jnp.sum((part >= 0).astype(jnp.float32), axis=1, keepdims=True).astype(jnp.int32)
+        begin = table[:, odd * REACH : odd * REACH + 1].astype(jnp.int32) - ids
+        begin = jnp.where(begin < 0, begin + tiles, begin)
+        behind = device - index
+        hit = known & (behind >= begin) & (behind < begin + named)
+        parity.append((index, ids, named, hit))
+    plans = []
+    for row in (REACH + core, REACH + 1 - core):
+        target = tile - core + row - REACH
+        live, rank, extra = 0, 0, 0
+        for index, ids, named, hit in parity:
+            live += (hit & (index == row)).astype(jnp.int32)
+            rank += (hit & (ids < target)).astype(jnp.int32)
+            extra += jnp.where((index == row) & (lane == 0), named, 0)
+        live = jnp.sum(live.astype(jnp.float32), axis=0, keepdims=True)
+        rank = jnp.sum(rank.astype(jnp.float32), axis=0, keepdims=True)
+        weight = jnp.zeros((1, table.shape[1]), jnp.float32)
+        for step in range(5):
+            weight = jnp.where(lane[:1] == step, float(8**step), weight)
+        packed = jnp.sum(weight * live * (rank + 1.0))
+        plans.append((packed.astype(jnp.int32), jnp.sum(extra.astype(jnp.float32))))
+    return plans
+
+
+def slot_kernel(*refs, members, ring):
+    if ring:
+        behind_ref = None
+    else:
+        behind_ref, *refs = refs
+    (
+        near_ref,
+        far2_ref,
+        far4_ref,
+        far6_ref,
+        far8_ref,
+        mine_ref,
+        theirs_ref,
+        base_ref,
+        in_ref,
+        mid_ref,
+        out_ref,
+        own_ref,
+        peer_ref,
+        noise_ref,
+        sample_ref,
+        where_ref,
+    ) = refs
     records = (near_ref, far2_ref, far4_ref, far6_ref, far8_ref)
+    blocks = [record[record.shape[0] - 1].astype(jnp.float32) for record in records]
+    ahead = [block[0:1] for block in blocks]
+    if ring:
+        behind = [ahead[4]] + [block[1:2] for block in blocks[1:4]]
+    else:
+        behind = [behind_ref[0:4].astype(jnp.float32)]
+    spare = jnp.full((7, near_ref.shape[2]), -1.0, jnp.float32)
+    table = jnp.concatenate(behind + ahead + [spare], axis=0)
+    plans = slot_plan(table, lax.axis_index("tile"), lax.axis_size("tile"))
     channels, cells = mine_ref.shape
     rows, width = noise_ref.shape[2:]
-
-    def names(table, device):
-        first = routes_ref[table * REACH]
-        place = lax.rem(device - first + tiles, tiles)
-        entry = routes_ref[table * REACH + jnp.minimum(place, REACH - 1)]
-        return (first >= 0) & (place < REACH) & (entry >= 0)
-
-    def members_of(table):
-        return 4 + sum((routes_ref[table * REACH + j] >= 0).astype(jnp.int32) for j in range(REACH))
-
-    own_row = REACH + core
-    peer_row = REACH + 1 - core
-    found = []
-    for step in range(5):
-        device_row = own_row + 2 * step
-        device = lax.rem(tile + 2 * step, tiles)
-        source_tiles, named = [], []
-        for back in range(REACH):
-            row = device_row - back
-            source_tiles.append(lax.rem(chip_tile + row - REACH + tiles, tiles))
-            named.append(names(row, device))
-        for side, row in ((0, own_row), (1, peer_row)):
-            back = device_row - row
-            inside = (back >= 0) & (back < REACH)
-            target = lax.rem(chip_tile + row - REACH, tiles)
-            live = jnp.int32(0)
-            rank = jnp.int32(0)
-            for at in range(REACH):
-                live = live | ((back == at) & named[at]).astype(jnp.int32)
-                rank = rank + (named[at] & (source_tiles[at] < target)).astype(jnp.int32)
-            found.append((step, side, inside & (live == 1), rank))
-
     count = jnp.int32(0)
-    for step, side, live, rank in found:
-        place = count
-
-        @pl.when(live)
-        def _():
-            noise_ref[place] = records[step][pl.ds(channels * rank, channels)]
-            where_ref[place] = side
-
-        count = count + live.astype(jnp.int32)
-
-    own_scale = 1.0 / members_of(own_row).astype(jnp.float32)
-    peer_scale = 1.0 / members_of(peer_row).astype(jnp.float32)
+    for side, (packed, _) in enumerate(plans):
+        for step, record in enumerate(records):
+            digit = lax.shift_right_logical(packed, 3 * step) & 7
+            place = count
+
+            @pl.when(digit > 0)
+            def _():
+                noise_ref[place] = record[pl.ds(channels * (digit - 1), channels)]
+                where_ref[place] = side
+
+            count = count + (digit > 0).astype(jnp.int32)
+
+    own_scale, peer_scale = [1.0 / (members + extra) for _, extra in plans]
     sample_ref[0] = base_ref[...]
     sample_ref[1] = jnp.zeros_like(base_ref)
     w_in, w_mid, w_out = in_ref[...], mid_ref[...], out_ref[...]
@@ -311,31 +329,40 @@
     step_flops = 2 * NSTEP * hidden * (hidden + 3 * channels)
     params = pltpu.CompilerParams(vmem_limit_bytes=VMEM_LIMIT)
 
+    peer_routes = swap_cores(extra_dest)
+    even = jnp.where(tile % 2 == 0, extra_dest, peer_routes)
+    odd = jnp.where(tile % 2 == 0, peer_routes, extra_dest)
+    chip_routes = jnp.concatenate([even, odd], axis=1)
     edge = edge_rows(coarse, section)
     half_noise = lax.dynamic_slice_in_dim(slot_noise, rows * section, rows, axis=2)
     half_noise = half_noise.reshape(slots * channels, rows, width)
 
     def record_of(routes):
-        block = jnp.pad(routes.astype(jnp.bfloat16), ((0, rows - routes.shape[0]), (0, width - REACH)))
+        pads = ((0, rows - routes.shape[0]), (0, width - 2 * REACH))
+        block = jnp.pad(routes.astype(jnp.bfloat16), pads)
         return jnp.concatenate([half_noise, block[None]], axis=0)
 
-    far8 = from_ahead(record_of(extra_dest), 8)
+    def routes_of(record, row):
+        return record[-1, row : row + 1, : 2 * REACH].astype(jnp.int32)
+
+    far8 = from_ahead(record_of(chip_routes), 8)
 
     weight = jax.ShapeDtypeStruct((2 * channels, hidden), jnp.bfloat16)
-    condition, w_in, w_mid = pl.pallas_call(
+    condition, w_in, w_mid, w_out = pl.pallas_call(
         regress_kernel,
         out_shape=(
             jax.ShapeDtypeStruct((channels, cells), jnp.bfloat16),
             weight,
-            jax.ShapeDtypeStruct((hidden, hidden), jnp.bfloat16),
+            jax.ShapeDtypeStruct(denoise_mid.shape, jnp.bfloat16),
+            jax.ShapeDtypeStruct(denoise_out.shape, jnp.bfloat16),
         ),
-        in_specs=in_vmem(2) + [pl.BlockSpec(memory_space=pl.ANY)] * 5,
-        out_specs=(pl.BlockSpec(memory_space=pltpu.VMEM),) * 3,
+        in_specs=in_vmem(2) + [pl.BlockSpec(memory_space=pltpu.HBM)] * 6,
+        out_specs=(pl.BlockSpec(memory_space=pltpu.VMEM),) * 4,
         scratch_shapes=[
             pltpu.VMEM((coarse.shape[0], hidden), jnp.bfloat16),
             pltpu.VMEM(conv_weight.shape, jnp.bfloat16),
             pltpu.VMEM(out_weight.shape, jnp.bfloat16),
-            pltpu.SemaphoreType.DMA((5,)),
+            pltpu.SemaphoreType.DMA((6,)),
         ],
         compiler_params=params,
         cost_estimate=pl.CostEstimate(
@@ -344,24 +371,18 @@
             transcendentals=2 * cells * hidden,
         ),
         name="regression",
-    )(coarse, edge, lift_weight.T, conv_weight, out_weight, denoise_in.T, denoise_mid)
+    )(coarse, edge, lift_weight.T, conv_weight, out_weight, denoise_in.T, denoise_mid, denoise_out)
 
     far8_after, condition = lax.optimization_barrier((far8, condition))
-    far8_routes = far8_after[-1, :1, :REACH].astype(jnp.int32)
-    record = record_of(jnp.concatenate([extra_dest, far8_routes], axis=0))
+    record = record_of(jnp.concatenate([chip_routes, routes_of(far8_after, 0)], axis=0))
     far2, far4, far6 = [from_ahead(record, distance) for distance in (2, 4, 6)]
-    got = [r[-1, :2, :REACH].astype(jnp.int32) for r in (far2, far4, far6)]
-    if count == 2 * REACH:
-        behind = [far8_routes[0], got[0][1], got[1][1], got[2][1]]
-    else:
-        behind = [from_ahead(extra_dest, -distance)[0] for distance in (8, 6, 4, 2)]
-    ahead = [extra_dest[0], got[0][0], got[1][0], got[2][0], far8_routes[0]]
-    own_routes = jnp.stack(behind + ahead)
     peer_condition = swap_cores(condition)
-    peer_routes = swap_cores(own_routes)
-    even = jnp.where(tile % 2 == 0, own_routes, peer_routes)
-    odd = jnp.where(tile % 2 == 0, peer_routes, own_routes)
-    routes = jnp.stack([even, odd], axis=1).reshape(-1)
+    ring = count == 2 * REACH
+    behind = []
+    if not ring:
+        block = [from_ahead(chip_routes, -distance) for distance in (8, 6, 4, 2)]
+        block = jnp.concatenate(block, axis=0).astype(jnp.bfloat16)
+        behind = [jnp.pad(block, ((0, rows - 4), (0, width - 2 * REACH)))]
 
     base = pl.pallas_call(
         base_kernel,
@@ -375,13 +396,13 @@
             transcendentals=2 * NSTEP * members * cells * hidden,
         ),
         name="base_members",
-    )(base_noise, condition, w_in, w_mid, denoise_out)
+    )(base_noise, condition, w_in, w_mid, w_out)
 
     moments = jax.ShapeDtypeStruct((2, channels, rows, width), jnp.float32)
     own, peer = pl.pallas_call(
-        slot_kernel,
+        functools.partial(slot_kernel, members=members, ring=ring),
         out_shape=(moments, moments),
-        in_specs=[pl.BlockSpec(memory_space=pltpu.SMEM)] + in_vmem(11),
+        in_specs=in_vmem(11 + len(behind)),
         out_specs=(pl.BlockSpec(memory_space=pltpu.VMEM),) * 2,
         scratch_shapes=[
             pltpu.VMEM((12, channels, rows, width), jnp.bfloat16),
@@ -396,8 +417,8 @@
         ),
         name="slot_members",
     )(
-        routes,
-        half_noise,
+        *behind,
+        record,
         far2,
         far4,
         far6,
@@ -407,7 +428,7 @@
         base,
         w_in,
         w_mid,
-        denoise_out,
+        w_out,
     )
     total = own + swap_cores(peer)
     mean = total[0]

time: 49.7 us -> 45.7 us (0.920)
  waiting for transfers between devices: 8.29 us -> 6.11 us
  local copies, waits for them, and re-layouts: 3.64 us -> 2.27 us
  Pallas kernels: 21.1 us -> 20.4 us
    ppermute x4, waiting for transfers between devices: 2.88 us -> 0.01 us  [from_ahead(): lax.ppermute(block, 'tile', [((i + distance) % count, i) for i in range(c...]
    unnamed x20, local copies, waits for them, and re-layouts: 3.22 us -> 2.25 us
    pallas_call x1, Pallas kernels: 10.3 us -> 9.59 us  [body(): pl.pallas_call(functools.partial(slot_kernel, members=members, ring=ring)...]
  transfers between devices with their start and end apart: 9 -> 9, of which waited for: 5 -> 4; matrix products, arithmetic and copies ran while one was open for 1% -> 0% of each run, Pallas kernels for 22% -> 24%
where the time goes in v2:
time: 45.7 us; the launch traced here: 45.4 us
  Pallas kernels  20.4 us (45%)
  starting transfers between devices  15.7 us (34%)
  waiting for transfers between devices  6.11 us (13%)
  local copies, waits for them, and re-layouts  2.27 us (5%)
  other arithmetic  0.8 us (2%)
    ppermute x4, starting transfers between devices, from_ahead(): lax.ppermute(block, 'tile', [((i + distance) % count, i) for i in range(c...  13 us
    pallas_call x1, Pallas kernels, body(): pl.pallas_call(functools.partial(slot_kernel, members=members, ring=ring)...  9.59 us
    pallas_call x1, Pallas kernels, body(): pl.pallas_call(base_kernel, out_shape=jax.ShapeDtypeStruct((2, channels,...  8.7 us
    ppermute x1, waiting for transfers between devices, swap_sections(): return lax.ppermute(block, 'section', [(0, 1), (1, 0)])  3.9 us
    unnamed x20, local copies, waits for them, and re-layouts  2.25 us
    pallas_call x1, Pallas kernels, body(): pl.pallas_call(regress_kernel, out_shape=(jax.ShapeDtypeStruct((channels,...  2.12 us
    ppermute x1, starting transfers between devices, edge_rows(): lax.ppermute(jnp.where(section == 0, last, first), ('section', 'tile'), p...  1.53 us
    ppermute x3, waiting for transfers between devices, swap_cores(): return lax.ppermute(block, 'tile', [(i, i ^ 1) for i in range(count)])  1.39 us
  transfers between devices with their start and end apart: 9, of which 4 were waited for; matrix products, arithmetic and copies ran while one was open for 0% of the time, Pallas kernels for 24%

profile of v2, /device:TPU:0, one launch (start us, length us, event | category | flops | bytes accessed | tf_op | source)
XLA Modules:
  0.0 45.4 jit_solution(16370859480953533025)
XLA Ops:
  0.0 0.0 copy-start
  0.0 0.5 collective-permute-start
  0.5 0.4 copy-done
  0.9 0.0 copy-start.9
  0.9 0.0 copy-start.1
  0.9 0.5 %collective-permute-done = s32[1,8]{1,0:T(1,128)S(1)} collective-permute-done((s32[1,8]{1,0:T(1,128)}, s32[1,8]{1,0:T(1,128)S(1)}, u32[]{:S(2)}, u32[]{:S(2)}) %collective-permute-start) | collective-permute-done | bytes 64 | tf_op jit(solution)/shard_map/ppermute | solution.py:293
  1.4 0.2 copy-done.9
  1.6 0.1 add_convert_fusion
  1.7 0.0 copy-start.4
  1.7 0.0 copy-start.5
  1.7 4.1 %collective-permute-start.1 = (bf16[17,16,128]{2,1,0:T(8,128)(2,1)S(1)}, bf16[17,16,128]{2,1,0:T(8,128)(2,1)S(1)}, u32[]{:S(2)}, u32[]{:S(2)}) collective-permute-start(bf16[17,16,128]{2,1,0:T(8,128)(2,1)S(1)} %pad_maximum_fusion), channel_id=1, source_target_pairs={{8,0},{9,1},{10,2},{11,3},{12,4},{13,5},{14,6},{15,7},{0,8},{1,9},... | collective-permute-start | bytes 208904 | tf_op jit(solution)/shard_map/ppermute | solution.py:288
  5.8 0.0 copy-done.1
  5.8 0.0 copy-start.8
  5.8 0.0 copy-start.6
  5.8 1.5 %collective-permute-start.2 = (bf16[12,1,128]{2,1,0:T(2,128)(2,1)S(1)}, bf16[12,1,128]{2,1,0:T(2,128)(2,1)S(1)}, u32[]{:S(2)}, u32[]{:S(2)}) collective-permute-start(bf16[12,1,128]{2,1,0:T(2,128)(2,1)S(1)} %broadcast_select_fusion.2), channel_id=1, source_target_pairs={{0,1},{1,2},{2,3},{3,4},{4,5},{5,6},{6,7},{7,8},{8,9},{9,10},{10,1... | collective-permute-start | bytes 9224 | tf_op jit(solution)/shard_map/ppermute | solution.py:306
  7.4 0.8 %collective-permute-done.2.edge_ref = bf16[12,1,128]{2,1,0:T(2,128)(2,1)S(1)} collective-permute-done((bf16[12,1,128]{2,1,0:T(2,128)(2,1)S(1)}, bf16[12,1,128]{2,1,0:T(2,128)(2,1)S(1)}, u32[]{:S(2)}, u32[]{:S(2)}) %collective-permute-start.2) | collective-permute-done | bytes 3104 | tf_op jit(solution)/shard_map/ppermute | solution.py:306
  8.2 0.0 copy-start.7
  8.2 0.0 copy-done.4
  8.2 0.0 copy-done.5
  8.2 0.0 copy-done.8
  8.2 0.0 copy-done.6
  8.2 0.7 %copy-done.7 = bf16[4,128]{1,0:T(4,128)(2,1)S(1)} copy-done((bf16[4,128]{1,0:T(4,128)(2,1)S(1)}, bf16[4,128]{1,0:T(4,128)(2,1)}, u32[]{:S(2)}) %copy-start.7) | copy-done | bytes 1048
  8.9 0.0 copy-start.2
  8.9 1.0 %copy-done.2 = bf16[3,3,128,128]{3,2,1,0:T(8,128)(2,1)S(1)} copy-done((bf16[3,3,128,128]{3,2,1,0:T(8,128)(2,1)S(1)}, bf16[3,3,128,128]{3,2,1,0:T(8,128)(2,1)}, u32[]{:S(2)}) %copy-start.2) | copy-done | bytes 294936
  9.8 2.1 %regression.1 = (bf16[4,2048]{1,0:T(4,128)(2,1)S(1)}, bf16[8,128]{1,0:T(8,128)(2,1)S(1)}, bf16[128,128]{1,0:T(8,128)(2,1)S(1)}, bf16[4,128]{1,0:T(4,128)(2,1)S(1)}) custom-call(bf16[12,32,128]{2,1,0:T(8,128)(2,1)S(1)} %copy-done.1, bf16[12,1,128]{2,1,0:T(2,128)(2,1)S(1)} %collective-permute-done.2.edge_ref, bf16[12,128]{1,0:T(8,128)(2,1)S(1)} %bitcast.33, ...), custom_call_target="tpu_custom_call" | custom-call | flops 612368384 | bytes 600000 | tf_op jit(solution)/shard_map/regression/pallas_call | solution.py:351
  11.9 0.0 copy-start.3
  12.0 0.0 collective-permute-done.1.refs_4_
  12.0 3.9 %collective-permute-start.5 = (bf16[17,16,128]{2,1,0:T(8,128)(2,1)S(1)}, bf16[17,16,128]{2,1,0:T(8,128)(2,1)S(1)}, u32[]{:S(2)}, u32[]{:S(2)}) collective-permute-start(bf16[17,16,128]{2,1,0:T(8,128)(2,1)S(1)} %pad_maximum_fusion.1.refs_0_), channel_id=1, source_target_pairs={{6,0},{7,1},{8,2},{9,3},{10,4},{11,5},{12,6},{13,7},{14,8},{15,9},... | collective-permute-start | bytes 208904 | tf_op jit(solution)/shard_map/ppermute | solution.py:288
  16.0 3.6 %collective-permute-start.4 = (bf16[17,16,128]{2,1,0:T(8,128)(2,1)S(1)}, bf16[17,16,128]{2,1,0:T(8,128)(2,1)S(1)}, u32[]{:S(2)}, u32[]{:S(2)}) collective-permute-start(bf16[17,16,128]{2,1,0:T(8,128)(2,1)S(1)} %pad_maximum_fusion.1.refs_0_), channel_id=1, source_target_pairs={{4,0},{5,1},{6,2},{7,3},{8,4},{9,5},{10,6},{11,7},{12,8},{13,9},{1... | collective-permute-start | bytes 208904 | tf_op jit(solution)/shard_map/ppermute | solution.py:288
  19.6 1.4 %collective-permute-start.3 = (bf16[17,16,128]{2,1,0:T(8,128)(2,1)S(1)}, bf16[17,16,128]{2,1,0:T(8,128)(2,1)S(1)}, u32[]{:S(2)}, u32[]{:S(2)}) collective-permute-start(bf16[17,16,128]{2,1,0:T(8,128)(2,1)S(1)} %pad_maximum_fusion.1.refs_0_), channel_id=1, source_target_pairs={{2,0},{3,1},{4,2},{5,3},{6,4},{7,5},{8,6},{9,7},{10,8},{11,9},{12,... | collective-permute-start | bytes 208904 | tf_op jit(solution)/shard_map/ppermute | solution.py:288
  21.0 0.0 collective-permute-start.6
  21.0 0.0 copy-done.3
  21.0 8.7 %base_members.1.refs_7_ = f32[2,4,2048]{2,1,0:T(4,128)S(1)} custom-call(bf16[4,4,32,128]{3,2,1,0:T(8,128)(2,1)S(1)} %copy-done.3, bf16[4,2048]{1,0:T(4,128)(2,1)S(1)} %get-tuple-element.15.condition_ref.refs_5_, bf16[8,128]{1,0:T(8,128)(2,1)S(1)} %get-tuple-element.16.in_ref.refs_8_, bf16[128,128]{1,0:T(8,128)(2,1)S(1)} %get-tuple-element.17.mid_ref.refs_9_, ...), custom_call_target="tpu_custom_call" | custom-call | flops 1761607680 | bytes 400000 | tf_op jit(solution)/shard_map/base_members/pallas_call | solution.py:387
  29.7 0.0 collective-permute-done.6.refs_6_
  29.7 0.0 collective-permute-done.5.refs_3_
  29.7 0.0 collective-permute-done.4.refs_2_
  29.7 0.0 collective-permute-done.3.refs_1_
  29.7 9.6 %slot_members.1 = (f32[2,4,16,128]{3,2,1,0:T(8,128)S(1)}, f32[2,4,16,128]{3,2,1,0:T(8,128)S(1)}) custom-call(bf16[17,16,128]{2,1,0:T(8,128)(2,1)S(1)} %pad_maximum_fusion.1.refs_0_, bf16[17,16,128]{2,1,0:T(8,128)(2,1)S(1)} %collective-permute-done.3.refs_1_, bf16[17,16,128]{2,1,0:T(8,128)(2,1)S(1)} %collective-permute-done.4.refs_2_, ...), custom_call_target="tpu_custom_call" | custom-call | flops 1761607680 | bytes 1000000 | tf_op jit(solution)/shard_map/slot_members/pallas_call | solution.py:402
  39.3 0.6 %collective-permute-start.7 = (f32[2,4,16,128]{3,2,1,0:T(8,128)S(1)}, f32[2,4,16,128]{3,2,1,0:T(8,128)S(1)}, u32[]{:S(2)}, u32[]{:S(2)}) collective-permute-start(f32[2,4,16,128]{3,2,1,0:T(8,128)S(1)} %get-tuple-element.20), channel_id=1, source_target_pairs={{0,1},{1,0},{2,3},{3,2},{4,5},{5,4},{6,7},{7,6},{8,9},{9,8},{10,11... | collective-permute-start | bytes 196616 | tf_op jit(solution)/shard_map/ppermute | solution.py:293
  39.9 0.9 %collective-permute-done.7 = f32[2,4,16,128]{3,2,1,0:T(8,128)S(1)} collective-permute-done((f32[2,4,16,128]{3,2,1,0:T(8,128)S(1)}, f32[2,4,16,128]{3,2,1,0:T(8,128)S(1)}, u32[]{:S(2)}, u32[]{:S(2)}) %collective-permute-start.7) | collective-permute-done | bytes 65568 | tf_op jit(solution)/shard_map/ppermute | solution.py:293
  40.8 0.1 collective-permute-start.8
  40.9 3.9 %collective-permute-done.8 = f32[4,16,128]{2,1,0:T(8,128)S(1)} collective-permute-done((f32[4,16,128]{2,1,0:T(8,128)S(1)}, f32[4,16,128]{2,1,0:T(8,128)S(1)}, u32[]{:S(2)}, u32[]{:S(2)}) %collective-permute-start.8) | collective-permute-done | bytes 32800 | tf_op jit(solution)/shard_map/ppermute | solution.py:297
  44.8 0.6 %maximum_bitcast_fusion = f32[1,4,32,128]{3,2,1,0:T(8,128)} fusion(f32[4,16,128]{2,1,0:T(8,128)S(1)} %get-tuple-element.22, f32[4,16,128]{2,1,0:T(8,128)S(1)} %get-tuple-element.21), kind=kLoop, calls=%fused_computation.2 | loop fusion | flops 16384 | bytes 131072 | tf_op jit(solution)/shard_map/broadcast_in_dim | solution.py:441
  (11 shorter events, 0.1 us)
Async XLA Ops:
  0.0 0.9 %copy-start = (bf16[4,4,32,128]{3,2,1,0:T(8,128)(2,1)S(1)}, bf16[4,4,32,128]{3,2,1,0:T(8,128)(2,1)}, u32[]{:S(2)}) copy-start(bf16[4,4,32,128]{3,2,1,0:T(8,128)(2,1)} %param.18) | copy-start | bytes 393220
  0.0 1.4 %collective-permute-start = (s32[1,8]{1,0:T(1,128)}, s32[1,8]{1,0:T(1,128)S(1)}, u32[]{:S(2)}, u32[]{:S(2)}) collective-permute-start(s32[1,8]{1,0:T(1,128)} %param.19), channel_id=1, source_target_pairs={{0,1},{1,0},{2,3},{3,2},{4,5},{5,4},{6,7},{7,6},{8,9},{9,8},{10,11... | collective-permute-start | bytes 104 | tf_op jit(solution)/shard_map/ppermute | solution.py:293
  0.9 0.7 %copy-start.9 = (s32[1,8]{1,0:T(1,128)S(1)}, s32[1,8]{1,0:T(1,128)}, u32[]{:S(2)}) copy-start(s32[1,8]{1,0:T(1,128)} %param.19) | copy-start | bytes 100
  0.9 4.9 %copy-start.1 = (bf16[12,32,128]{2,1,0:T(8,128)(2,1)S(1)}, bf16[12,32,128]{2,1,0:T(8,128)(2,1)}, u32[]{:S(2)}) copy-start(bf16[12,32,128]{2,1,0:T(8,128)(2,1)} %coarse_ref.1) | copy-start | bytes 294916
  1.7 6.5 %copy-start.4 = (bf16[128,128]{1,0:T(8,128)(2,1)S(1)}, bf16[128,128]{1,0:T(8,128)(2,1)}, u32[]{:S(2)}) copy-start(bf16[128,128]{1,0:T(8,128)(2,1)} %mid_hbm.1) | copy-start | bytes 98308
  1.7 6.5 %copy-start.5 = (bf16[128,12]{0,1:T(8,128)(2,1)S(1)}, bf16[128,12]{0,1:T(8,128)(2,1)}, u32[]{:S(2)}) copy-start(bf16[128,12]{0,1:T(8,128)(2,1)} %param.11) | copy-start | bytes 9220
  1.7 10.3 %collective-permute-start.1 = (bf16[17,16,128]{2,1,0:T(8,128)(2,1)S(1)}, bf16[17,16,128]{2,1,0:T(8,128)(2,1)S(1)}, u32[]{:S(2)}, u32[]{:S(2)}) collective-permute-start(bf16[17,16,128]{2,1,0:T(8,128)(2,1)S(1)} %pad_maximum_fusion), channel_id=1, source_target_pairs={{8,0},{9,1},{10,2},{11,3},{12,4},{13,5},{14,6},{15,7},{0,8},{1,9},... | collective-permute-start | bytes 208904 | tf_op jit(solution)/shard_map/ppermute | solution.py:288
  5.8 2.4 %copy-start.8 = (bf16[4,128]{1,0:T(4,128)(2,1)S(1)}, bf16[4,128]{1,0:T(4,128)(2,1)}, u32[]{:S(2)}) copy-start(bf16[4,128]{1,0:T(4,128)(2,1)} %last_hbm.1) | copy-start | bytes 3076
  5.8 2.4 %copy-start.6 = (bf16[128,8]{0,1:T(8,128)(2,1)S(1)}, bf16[128,8]{0,1:T(8,128)(2,1)}, u32[]{:S(2)}) copy-start(bf16[128,8]{0,1:T(8,128)(2,1)} %param.14) | copy-start | bytes 6148
  5.8 2.3 %collective-permute-start.2 = (bf16[12,1,128]{2,1,0:T(2,128)(2,1)S(1)}, bf16[12,1,128]{2,1,0:T(2,128)(2,1)S(1)}, u32[]{:S(2)}, u32[]{:S(2)}) collective-permute-start(bf16[12,1,128]{2,1,0:T(2,128)(2,1)S(1)} %broadcast_select_fusion.2), channel_id=1, source_target_pairs={{0,1},{1,2},{2,3},{3,4},{4,5},{5,6},{6,7},{7,8},{8,9},{9,10},{10,1... | collective-permute-start | bytes 9224 | tf_op jit(solution)/shard_map/ppermute | solution.py:306
  8.2 0.7 %copy-start.7 = (bf16[4,128]{1,0:T(4,128)(2,1)S(1)}, bf16[4,128]{1,0:T(4,128)(2,1)}, u32[]{:S(2)}) copy-start(bf16[4,128]{1,0:T(4,128)(2,1)} %out_hbm.1) | copy-start | bytes 3076
  8.9 1.0 %copy-start.2 = (bf16[3,3,128,128]{3,2,1,0:T(8,128)(2,1)S(1)}, bf16[3,3,128,128]{3,2,1,0:T(8,128)(2,1)}, u32[]{:S(2)}) copy-start(bf16[3,3,128,128]{3,2,1,0:T(8,128)(2,1)} %conv_hbm.1) | copy-start | bytes 884740
  11.9 9.0 %copy-start.3 = (bf16[4,4,32,128]{3,2,1,0:T(8,128)(2,1)S(1)}, bf16[4,4,32,128]{3,2,1,0:T(8,128)(2,1)}, u32[]{:S(2)}) copy-start(bf16[4,4,32,128]{3,2,1,0:T(8,128)(2,1)} %noise_ref.1) | copy-start | bytes 393220
  12.0 17.7 %collective-permute-start.5 = (bf16[17,16,128]{2,1,0:T(8,128)(2,1)S(1)}, bf16[17,16,128]{2,1,0:T(8,128)(2,1)S(1)}, u32[]{:S(2)}, u32[]{:S(2)}) collective-permute-start(bf16[17,16,128]{2,1,0:T(8,128)(2,1)S(1)} %pad_maximum_fusion.1.refs_0_), channel_id=1, source_target_pairs={{6,0},{7,1},{8,2},{9,3},{10,4},{11,5},{12,6},{13,7},{14,8},{15,9},... | collective-permute-start | bytes 208904 | tf_op jit(solution)/shard_map/ppermute | solution.py:288
  16.0 13.7 %collective-permute-start.4 = (bf16[17,16,128]{2,1,0:T(8,128)(2,1)S(1)}, bf16[17,16,128]{2,1,0:T(8,128)(2,1)S(1)}, u32[]{:S(2)}, u32[]{:S(2)}) collective-permute-start(bf16[17,16,128]{2,1,0:T(8,128)(2,1)S(1)} %pad_maximum_fusion.1.refs_0_), channel_id=1, source_target_pairs={{4,0},{5,1},{6,2},{7,3},{8,4},{9,5},{10,6},{11,7},{12,8},{13,9},{1... | collective-permute-start | bytes 208904 | tf_op jit(solution)/shard_map/ppermute | solution.py:288
  19.6 10.1 %collective-permute-start.3 = (bf16[17,16,128]{2,1,0:T(8,128)(2,1)S(1)}, bf16[17,16,128]{2,1,0:T(8,128)(2,1)S(1)}, u32[]{:S(2)}, u32[]{:S(2)}) collective-permute-start(bf16[17,16,128]{2,1,0:T(8,128)(2,1)S(1)} %pad_maximum_fusion.1.refs_0_), channel_id=1, source_target_pairs={{2,0},{3,1},{4,2},{5,3},{6,4},{7,5},{8,6},{9,7},{10,8},{11,9},{12,... | collective-permute-start | bytes 208904 | tf_op jit(solution)/shard_map/ppermute | solution.py:288
  21.0 8.7 %collective-permute-start.6 = (bf16[4,2048]{1,0:T(4,128)(2,1)S(1)}, bf16[4,2048]{1,0:T(4,128)(2,1)S(1)}, u32[]{:S(2)}, u32[]{:S(2)}) collective-permute-start(bf16[4,2048]{1,0:T(4,128)(2,1)S(1)} %get-tuple-element.15.condition_ref.refs_5_), channel_id=1, source_target_pairs={{0,1},{1,0},{2,3},{3,2},{4,5},{5,4},{6,7},{7,6},{8,9},{9,8},{10,11... | collective-permute-start | bytes 49160 | tf_op jit(solution)/shard_map/ppermute | solution.py:293
  39.3 1.5 %collective-permute-start.7 = (f32[2,4,16,128]{3,2,1,0:T(8,128)S(1)}, f32[2,4,16,128]{3,2,1,0:T(8,128)S(1)}, u32[]{:S(2)}, u32[]{:S(2)}) collective-permute-start(f32[2,4,16,128]{3,2,1,0:T(8,128)S(1)} %get-tuple-element.20), channel_id=1, source_target_pairs={{0,1},{1,0},{2,3},{3,2},{4,5},{5,4},{6,7},{7,6},{8,9},{9,8},{10,11... | collective-permute-start | bytes 196616 | tf_op jit(solution)/shard_map/ppermute | solution.py:293
  40.8 4.0 %collective-permute-start.8 = (f32[4,16,128]{2,1,0:T(8,128)S(1)}, f32[4,16,128]{2,1,0:T(8,128)S(1)}, u32[]{:S(2)}, u32[]{:S(2)}) collective-permute-start(f32[4,16,128]{2,1,0:T(8,128)S(1)} %fusion.1), channel_id=1, source_target_pairs={{0,16},{16,0},{1,17},{17,1},{2,18},{18,2},{3,19},{19,3},{4,20},{20... | collective-permute-start | bytes 98312 | tf_op jit(solution)/shard_map/ppermute | solution.py:297
